TPU v7x, 256 devices: a whole 4x4x8 slice. The times are simulated.
256 devices in a mesh: blk: 64 (over y_hi, z, x), span: 4 (over y_lo, core).
Axes of the slice: x: 4, y: 4 (y_hi: 2, y_lo: 2; y = y_hi * 2 + y_lo), z: 8, core: 2. Of those that a mesh axis runs over, the one named last changes fastest.
Arguments:
- home_table: float32 [400, 65536], P(None, ('blk', 'span')), may hold values from -3 to 3
- home_state: float32 [65536], P(('blk', 'span')), may hold values from 0.0001 to 1
- visit_table: float32 [400, 65536], P(None, ('blk', 'span')), may hold values from -3 to 3
- visit_state: float32 [65536], P(('blk', 'span')), may hold values from 0.0001 to 1
- relation_table: float32 [400, 7424], P(None, ('blk', 'span')), may hold values from -2 to 2
- relation_state: float32 [7424], P(('blk', 'span')), may hold values from 0.0001 to 1
- edge_src: int32 [64, 4, 1024], P('blk', 'span'), may hold values from 0 to 1023
- edge_rel: int32 [64, 4, 1024], P('blk', 'span'), may hold values from 0 to 7423
- edge_dst: int32 [64, 4, 1024], P('blk', 'span'), may hold values from 0 to 255
- edge_count: int32 [64, 4], P('blk', 'span'), may hold values from 65 to 1024, as said below
- neg_rows: int32 [64, 1024], P('blk'), may hold values from 0 to 1023
Outputs:
- new_home_table: float32 [400, 65536], P(None, ('blk', 'span'))
- new_home_state: float32 [65536], P(('blk', 'span'))
- new_visit_table: float32 [400, 65536], P(None, ('blk', 'span'))
- new_visit_state: float32 [65536], P(('blk', 'span'))
- new_relation_table: float32 [400, 7424], P(None, ('blk', 'span'))
- new_relation_state: float32 [7424], P(('blk', 'span'))
Inputs may be any that keep to these rules, and one draw needn't show every extreme that they name: `edge_count`: the counts of one bucket sum to at most 1536; some bucket reaches that sum and some span index reaches 1024.
All inputs are finite; a program needn't handle non-finite values.
Results may differ from a plain program's by a relative error of at most 0.0023.
Values may be sent and summed in bfloat16 or wider, within the bound.
A program may use at most 128 MiB of HBM per device.

v0:
```python
import jax
import jax.numpy as jnp
from jax import lax
from jax.sharding import PartitionSpec as P

LEARN_RATE = 0.1
ADAGRAD_EPS = 1e-10


def passed_along(value, axis, steps):
    count = lax.axis_size(axis)
    pairs = [(source, (source + steps) % count) for source in range(count)]
    return lax.ppermute(value, axis, pairs)


def complex_apply(left, right):
    middle = left.shape[0] // 2
    left_re = left[:middle].astype(jnp.float32)
    left_im = left[middle:].astype(jnp.float32)
    right_re = right[:middle].astype(jnp.float32)
    right_im = right[middle:].astype(jnp.float32)
    return jnp.concatenate(
        [left_re * right_re - left_im * right_im, left_re * right_im + left_im * right_re], axis=0
    )


def conj_apply(left, grad_in):
    middle = left.shape[0] // 2
    left_re = left[:middle].astype(jnp.float32)
    left_im = left[middle:].astype(jnp.float32)
    grad_re = grad_in[:middle]
    grad_im = grad_in[middle:]
    return jnp.concatenate(
        [left_re * grad_re + left_im * grad_im, left_re * grad_im - left_im * grad_re], axis=0
    )


def edge_grads(source, dest, relation, live_mask, negatives):
    trans = lax.optimization_barrier(complex_apply(relation, dest).astype(jnp.bfloat16))
    trans_wide = trans.astype(jnp.float32)
    positive = jnp.sum(source.astype(jnp.float32) * trans_wide, axis=0)
    neg_score = lax.dot_general(
        trans, negatives, (((0,), (0,)), ((), ())), preferred_element_type=jnp.float32
    )
    pos_weight = -live_mask * jax.nn.sigmoid(-positive)
    neg_weight = (live_mask[:, None] * jax.nn.sigmoid(neg_score) / negatives.shape[1]).astype(
        jnp.bfloat16
    )
    neg_pull = lax.dot_general(
        negatives, neg_weight, (((1,), (1,)), ((), ())), preferred_element_type=jnp.float32
    )
    grad_trans = pos_weight[None, :] * source.astype(jnp.float32) + neg_pull
    grad_source = pos_weight[None, :] * trans_wide
    grad_dest = conj_apply(relation, grad_trans)
    grad_relation = conj_apply(dest, grad_trans)
    grad_negative = jnp.dot(trans, neg_weight, preferred_element_type=jnp.float32)
    return (grad_source, grad_dest, grad_relation, grad_negative)


def adagrad(table, state, grad_in):
    state_new = state + jnp.mean(grad_in * grad_in, axis=0)
    return (table - LEARN_RATE * grad_in / (jnp.sqrt(state_new)[None, :] + ADAGRAD_EPS), state_new)


def block_rows():
    return 512


def score_slots(
    home_all,
    relation_all,
    negatives,
    source_rows,
    relation_ids,
    dest_vectors,
    live_mask,
    home_acc,
    relation_acc,
):
    features, total_rows = dest_vectors.shape
    step_rows = block_rows()

    def one_block(block_index, totals):
        home_total, relation_total, negative_total, dest_grads = totals
        first_row = block_index * step_rows
        source_part = lax.dynamic_slice_in_dim(source_rows, first_row, step_rows)
        relation_part = lax.dynamic_slice_in_dim(relation_ids, first_row, step_rows)
        live_part = lax.dynamic_slice_in_dim(live_mask, first_row, step_rows)
        dest_part = lax.dynamic_slice_in_dim(dest_vectors, first_row, step_rows, 1)
        grad_source, grad_dest, grad_relation, grad_negative = edge_grads(
            jnp.take(home_all, source_part, axis=1),
            dest_part,
            jnp.take(relation_all, relation_part, axis=1),
            live_part,
            negatives,
        )
        home_total = home_total.at[:, source_part].add(grad_source)
        relation_total = relation_total.at[:, relation_part].add(grad_relation)
        dest_grads = lax.dynamic_update_slice_in_dim(dest_grads, grad_dest, first_row, 1)
        return (home_total, relation_total, negative_total + grad_negative, dest_grads)

    initial = (
        home_acc,
        relation_acc,
        jnp.zeros((features, negatives.shape[1]), jnp.float32),
        jnp.zeros((features, total_rows), jnp.float32),
    )
    return lax.fori_loop(0, total_rows // step_rows, one_block, initial)


def shards(
    home_table,
    home_state,
    visit_table,
    visit_state,
    relation_table,
    relation_state,
    edge_src,
    edge_rel,
    edge_dst,
    edge_count,
    neg_rows,
):
    features, own_rows = home_table.shape
    slot_count = edge_src.shape[2]
    home_all = lax.all_gather(home_table.astype(jnp.bfloat16), "span", axis=1, tiled=True)
    relation_all = lax.all_gather(
        relation_table.astype(jnp.bfloat16), ("blk", "span"), axis=1, tiled=True
    )
    negatives = jnp.take(home_all, neg_rows[0], axis=1)
    visit_low = visit_table.astype(jnp.bfloat16)
    source_rows = edge_src[0, 0]
    relation_ids = edge_rel[0, 0]
    dest_rows = edge_dst[0, 0]
    live_flags = (jnp.arange(slot_count, dtype=jnp.int32) < edge_count[0, 0]).astype(jnp.int32)
    dest_vectors = jnp.take(visit_low, dest_rows, axis=1)
    home_acc = jnp.zeros((features, home_all.shape[1]), jnp.float32)
    relation_acc = jnp.zeros((features, relation_all.shape[1]), jnp.float32)
    home_acc, relation_acc, negative_total, dest_grads = score_slots(
        home_all,
        relation_all,
        negatives,
        source_rows,
        relation_ids,
        dest_vectors,
        live_flags.astype(jnp.float32),
        home_acc,
        relation_acc,
    )
    visit_grad = jnp.zeros((features, own_rows), jnp.float32).at[:, dest_rows].add(dest_grads)
    visit_updated, visit_state_updated = adagrad(visit_table, visit_state, visit_grad)
    moved_table, moved_state = passed_along((visit_updated, visit_state_updated), "blk", 1)
    home_acc = home_acc.at[:, neg_rows[0]].add(negative_total)
    home_grad = lax.psum_scatter(home_acc, "span", scatter_dimension=1, tiled=True)
    new_home, new_home_state = adagrad(home_table, home_state, home_grad)
    relation_grad = lax.psum_scatter(relation_acc, ("blk", "span"), scatter_dimension=1, tiled=True)
    new_relation, new_relation_state = adagrad(relation_table, relation_state, relation_grad)
    return (new_home, new_home_state, moved_table, moved_state, new_relation, new_relation_state)


def solution(mesh):
    placed = (
        P(None, ("blk", "span")),
        P(("blk", "span")),
        P(None, ("blk", "span")),
        P(("blk", "span")),
        P(None, ("blk", "span")),
        P(("blk", "span")),
        P("blk", "span", None),
        P("blk", "span", None),
        P("blk", "span", None),
        P("blk", "span"),
        P("blk", None),
    )
    return jax.shard_map(
        shards,
        mesh=mesh,
        in_specs=placed,
        out_specs=(
            P(None, ("blk", "span")),
            P(("blk", "span")),
            P(None, ("blk", "span")),
            P(("blk", "span")),
            P(None, ("blk", "span")),
            P(("blk", "span")),
        ),
        check_vma=False,
    )
```

profile of v0, /device:TPU:1, one launch (start us, length us, event | category | flops | bytes accessed | tf_op | source)
XLA Modules:
  0.0 1425.4 jit_solution(4683395752813671898)
XLA Ops:
  7.2 1.5 convert_bitcast_fusion
  9.8 10.4 all_gather.6
  20.8 4.0 gather_fusion.3
  27.0 4.0 gather_fusion.2
  33.7 399.3 %all-gather.3.cloned.1.call-done = bf16[256,29,400]{2,1,0:T(8,128)(2,1)} async-done(((bf16[1,29,400]{2,1,0:T(8,128)(2,1)}), bf16[256,29,400]{2,1,0:T(8,128)(2,1)}) %all-gather.3.cloned.1.call-update) | async-done | bytes 5939216 | tf_op jit(solution)/shard_map/all_gather | solution.py:127
  433.1 11.5 reshape.167
  444.6 7.3 broadcast_in_dim.80
  452.1 1.5 broadcast.129.clone.1
  453.6 116.5 %while.20 = (s32[]{:T(128)}, f32[400,1024]{0,1:T(8,128)S(1)}, f32[400,7424]{0,1:T(8,128)}, f32[400,1024]{1,0:T(8,128)}, f32[400,1024]{1,0:T(8,128)}, /*index=5*/...) while((s32[]{:T(128)}, f32[400,1024]{0,1:T(8,128)S(1)}, ...), condition=%wide.region_4.5_spmd.clone, body=%wide.region_0.4_spmd.clone.sunk | while | flops 1269229056 | bytes 48784400 | solution.py:108
  453.6 1.3 compare_and_fusion.5
  455.5 6.8 gather_fusion
  462.3 2.0 copy.85
  465.3 1.3 fusion.37
  467.9 2.8 gather_fusion.1
  470.7 2.0 copy.86
  474.6 2.3 multiply_convert_fusion.2
  480.6 2.5 copy.88
  483.0 14.9 %scatter_fusion.1 = f32[400,7424]{0,1:T(8,128)} fusion(f32[400,7424]{0,1:T(8,128)} %get-tuple-element.485, s32[512]{0:T(512)} %copy-done.11, f32[512,400]{1,0:T(8,128)} %copy.88), kind=kCustom, calls=%fused_computation.5.clone.clone.1 | custom fusion | flops 204800 | bytes 2459648 | tf_op jit(solution)/shard_map/while/body/eval_jaxpr/scatter-add | solution.py:98
  497.9 2.2 maximum_dynamic-update-slice_fusion.2
  500.0 3.0 select_add_fusion.2
  504.1 2.5 copy.87
  506.5 5.0 scatter_fusion
  511.6 1.3 compare_and_fusion.5
  513.5 6.8 gather_fusion
  520.3 2.0 copy.85
  523.3 1.3 fusion.37
  525.9 2.8 gather_fusion.1
  528.7 2.0 copy.86
  532.6 2.3 multiply_convert_fusion.2
  538.6 2.5 copy.88
  541.0 14.9 %scatter_fusion.1 = f32[400,7424]{0,1:T(8,128)} fusion(f32[400,7424]{0,1:T(8,128)} %get-tuple-element.485, s32[512]{0:T(512)} %copy-done.11, f32[512,400]{1,0:T(8,128)} %copy.88), kind=kCustom, calls=%fused_computation.5.clone.clone.1 | custom fusion | flops 204800 | bytes 2459648 | tf_op jit(solution)/shard_map/while/body/eval_jaxpr/scatter-add | solution.py:98
  555.9 2.1 maximum_dynamic-update-slice_fusion.2
  558.0 3.5 select_add_fusion.2
  562.5 2.5 copy.87
  565.0 5.0 scatter_fusion
  570.1 2.8 copy.72
  572.9 8.2 scatter_fusion.2
  582.5 716.6 %fusion = f32[400,32]{0,1:T(8,128)S(1)} fusion(f32[400,7424]{0,1:T(8,128)} %get-tuple-element.211), kind=kCustom, calls=%all-reduce-scatter | all-reduce-scatter fusion | flops 3276801 | bytes 11929600
  1299.1 1.3 collective-permute-start.10
  1300.4 1.3 collective-permute-start.11
  1301.7 1.3 collective-permute-start.12
  1303.0 1.3 collective-permute-start.25
  1304.3 1.8 copy.74
  1306.2 7.4 scatter_custom_fusion.3
  1313.8 8.1 collective-permute-done.1
  1323.2 1.3 collective-permute-start.14
  1324.5 1.3 collective-permute-start.15
  1325.8 1.3 collective-permute-start.16
  1327.1 1.3 collective-permute-start.17
  1328.5 1.3 collective-permute-start.18
  1329.8 1.3 collective-permute-start.19
  1331.1 1.9 collective-permute-start.2
  1333.0 1.3 collective-permute-start.20
  1334.3 1.3 collective-permute-start.21
  1335.6 1.3 collective-permute-start.22
  1337.0 2.6 collective-permute-start.23
  1339.6 31.5 %collective-permute-start.24 = (f32[400,32]{0,1:T(8,128)S(1)}, f32[400,32]{0,1:T(8,128)}, u32[]{:S(2)}, u32[]{:S(2)}) collective-permute-start(f32[400,32]{0,1:T(8,128)S(1)} %fusion), channel_id=1, source_target_pairs={{0,23},{1,24},{2,25},{3,26},{4,27},{5,28},{6,29},{7,30},{8,31},{9,... | collective-permute-start | bytes 153608
  1371.1 2.6 collective-permute-start.3
  1373.8 5.3 collective-permute-start.4
  1380.9 4.6 collective-permute-start.6
  1385.5 2.9 collective-permute-start.7
  1388.4 4.2 collective-permute-start.8
  1392.6 2.3 collective-permute-start.9
  1397.8 12.9 concatenate.25
  (174 shorter events, 40.5 us)
Async XLA Ops:
  7.2 13.6 copy-start.27
  7.2 425.9 %all-gather.3.cloned.1.call-start = ((), (), s32[]{:S(2)}) async-start(), calls=%async_computation.2 | async-start | bytes 8421376 | tf_op jit(solution)/shard_map/all_gather | solution.py:127
  8.7 1405.5 %reduce-scatter.4.cloned.1.call-start = ((), (), s32[]{:S(2)}) async-start(), calls=%async_computation.1 | async-start | bytes 2621440 | tf_op jit(solution)/shard_map/reduce_scatter | solution.py:154
  20.7 4.0 copy-start.25
  24.8 1.5 copy-start.8
  25.0 1.4 copy-start.28
  27.0 4.0 copy-start.29
  465.3 1.4 copy-start.1
  474.6 2.3 copy-start.13
  474.6 3.3 copy-start.3
  474.6 3.3 copy-start.10
  474.6 3.3 copy-start.24
  476.8 1.6 copy-start.2
  476.9 1.6 copy-start.4
  500.0 3.0 copy-start.14
  523.3 1.4 copy-start.1
  532.5 2.3 copy-start.13
  532.5 3.3 copy-start.3
  532.5 3.3 copy-start.10
  532.6 3.3 copy-start.24
  534.8 1.0 copy-start.5
  534.8 1.6 copy-start.2
  534.9 1.6 copy-start.4
  558.0 3.5 copy-start.14
  570.1 2.8 copy-start.26
  581.1 1.3 copy-start
  582.5 721.8 %copy-start.6 = (f32[400,1024]{1,0:T(8,128)S(1)}, f32[400,1024]{1,0:T(8,128)}, u32[]{:S(2)}) copy-start(f32[400,1024]{1,0:T(8,128)} %get-tuple-element.210) | copy-start | bytes 4915204
  1299.1 25.4 %collective-permute-start.10 = (f32[400,32]{0,1:T(8,128)S(1)}, f32[400,32]{0,1:T(8,128)S(1)}, u32[]{:S(2)}, u32[]{:S(2)}) collective-permute-start(f32[400,32]{0,1:T(8,128)S(1)} %fusion), channel_id=1, source_target_pairs={{0,9},{1,10},{2,11},{3,12},{4,13},{5,14},{6,15},{7,16},{8,17},{9,1... | collective-permute-start | bytes 153608
  1300.4 25.4 %collective-permute-start.11 = (f32[400,32]{0,1:T(8,128)S(1)}, f32[400,32]{0,1:T(8,128)S(1)}, u32[]{:S(2)}, u32[]{:S(2)}) collective-permute-start(f32[400,32]{0,1:T(8,128)S(1)} %fusion), channel_id=1, source_target_pairs={{0,10},{1,11},{2,12},{3,13},{4,14},{5,15},{6,16},{7,17},{8,18},{9,... | collective-permute-start | bytes 153608
  1301.7 25.5 %collective-permute-start.12 = (f32[400,32]{0,1:T(8,128)S(1)}, f32[400,32]{0,1:T(8,128)S(1)}, u32[]{:S(2)}, u32[]{:S(2)}) collective-permute-start(f32[400,32]{0,1:T(8,128)S(1)} %fusion), channel_id=1, source_target_pairs={{0,11},{1,12},{2,13},{3,14},{4,15},{5,16},{6,17},{7,18},{8,19},{9,... | collective-permute-start | bytes 153608
  1303.0 20.2 %collective-permute-start.25 = (f32[400,29]{0,1:T(8,128)S(1)}, f32[400,29]{0,1:T(8,128)S(1)}, u32[]{:S(2)}, u32[]{:S(2)}) collective-permute-start(f32[400,29]{0,1:T(8,128)S(1)} %slice.66), channel_id=1, source_target_pairs={{0,24},{1,25},{2,26},{3,27},{4,28},{5,29},{6,30},{7,31},{8,32},{9,... | collective-permute-start | bytes 139208
  1304.3 9.4 copy-start.31
  1304.3 74.8 %copy-start.7 = (f32[400,256]{1,0:T(8,128)S(1)}, f32[400,256]{1,0:T(8,128)}, u32[]{:S(2)}) copy-start(f32[400,256]{1,0:T(8,128)} %param.13) | copy-start | bytes 1228804
  1304.3 75.0 %copy-start.9 = (f32[400,256]{1,0:T(8,128)S(1)}, f32[400,256]{1,0:T(8,128)}, u32[]{:S(2)}) copy-start(f32[400,256]{1,0:T(8,128)} %param.15) | copy-start | bytes 1228804
  1313.7 8.2 collective-permute-start.1
  1321.9 6.5 collective-permute-start.13
  1323.2 6.5 collective-permute-start.14
  1324.5 6.5 collective-permute-start.15
  1325.8 7.2 collective-permute-start.16
  1327.1 7.2 collective-permute-start.17
  1328.5 7.2 collective-permute-start.18
  1329.8 7.2 collective-permute-start.19
  1331.1 8.5 collective-permute-start.2
  1333.0 38.1 %collective-permute-start.20 = (f32[400,32]{0,1:T(8,128)S(1)}, f32[400,32]{0,1:T(8,128)S(1)}, u32[]{:S(2)}, u32[]{:S(2)}) collective-permute-start(f32[400,32]{0,1:T(8,128)S(1)} %fusion), channel_id=1, source_target_pairs={{0,19},{1,20},{2,21},{3,22},{4,23},{5,24},{6,25},{7,26},{8,27},{9,... | collective-permute-start | bytes 153608
  1334.3 39.4 %collective-permute-start.21 = (f32[400,32]{0,1:T(8,128)S(1)}, f32[400,32]{0,1:T(8,128)S(1)}, u32[]{:S(2)}, u32[]{:S(2)}) collective-permute-start(f32[400,32]{0,1:T(8,128)S(1)} %fusion), channel_id=1, source_target_pairs={{0,20},{1,21},{2,22},{3,23},{4,24},{5,25},{6,26},{7,27},{8,28},{9,... | collective-permute-start | bytes 153608
  1335.6 43.9 %collective-permute-start.22 = (f32[400,32]{0,1:T(8,128)S(1)}, f32[400,32]{0,1:T(8,128)S(1)}, u32[]{:S(2)}, u32[]{:S(2)}) collective-permute-start(f32[400,32]{0,1:T(8,128)S(1)} %fusion), channel_id=1, source_target_pairs={{0,21},{1,22},{2,23},{3,24},{4,25},{5,26},{6,27},{7,28},{8,29},{9,... | collective-permute-start | bytes 153608
  1337.0 43.9 %collective-permute-start.23 = (f32[400,32]{0,1:T(8,128)S(1)}, f32[400,32]{0,1:T(8,128)S(1)}, u32[]{:S(2)}, u32[]{:S(2)}) collective-permute-start(f32[400,32]{0,1:T(8,128)S(1)} %fusion), channel_id=1, source_target_pairs={{0,22},{1,23},{2,24},{3,25},{4,26},{5,27},{6,28},{7,29},{8,30},{9,... | collective-permute-start | bytes 153608
  1339.6 55.2 %copy-start.15 = (f32[400,32]{0,1:T(8,128)}, f32[400,32]{0,1:T(8,128)S(1)}, u32[]{:S(2)}) copy-start(f32[400,32]{0,1:T(8,128)S(1)} %collective-permute-done.2) | copy-start | bytes 153604
  1339.6 45.9 %collective-permute-start.24 = (f32[400,32]{0,1:T(8,128)S(1)}, f32[400,32]{0,1:T(8,128)}, u32[]{:S(2)}, u32[]{:S(2)}) collective-permute-start(f32[400,32]{0,1:T(8,128)S(1)} %fusion), channel_id=1, source_target_pairs={{0,23},{1,24},{2,25},{3,26},{4,27},{5,28},{6,29},{7,30},{8,31},{9,... | collective-permute-start | bytes 153608
  1371.1 25.4 %copy-start.16 = (f32[400,32]{0,1:T(8,128)}, f32[400,32]{0,1:T(8,128)S(1)}, u32[]{:S(2)}) copy-start(f32[400,32]{0,1:T(8,128)S(1)} %collective-permute-done.20) | copy-start | bytes 153604
  1371.1 17.2 %collective-permute-start.3 = (f32[400,32]{0,1:T(8,128)S(1)}, f32[400,32]{0,1:T(8,128)}, u32[]{:S(2)}, u32[]{:S(2)}) collective-permute-start(f32[400,32]{0,1:T(8,128)S(1)} %fusion), channel_id=1, source_target_pairs={{0,2},{1,3},{2,4},{3,5},{4,6},{5,7},{6,8},{7,9},{8,10},{9,11},{10,... | collective-permute-start | bytes 153608
  1373.8 22.8 %copy-start.17 = (f32[400,32]{0,1:T(8,128)}, f32[400,32]{0,1:T(8,128)S(1)}, u32[]{:S(2)}) copy-start(f32[400,32]{0,1:T(8,128)S(1)} %collective-permute-done.21) | copy-start | bytes 153604
  1373.8 18.8 %collective-permute-start.4 = (f32[400,32]{0,1:T(8,128)S(1)}, f32[400,32]{0,1:T(8,128)}, u32[]{:S(2)}, u32[]{:S(2)}) collective-permute-start(f32[400,32]{0,1:T(8,128)S(1)} %fusion), channel_id=1, source_target_pairs={{0,3},{1,4},{2,5},{3,6},{4,7},{5,8},{6,9},{7,10},{8,11},{9,12},{10... | collective-permute-start | bytes 153608
  1379.5 17.0 %copy-start.18 = (f32[400,32]{0,1:T(8,128)}, f32[400,32]{0,1:T(8,128)S(1)}, u32[]{:S(2)}) copy-start(f32[400,32]{0,1:T(8,128)S(1)} %collective-permute-done.22) | copy-start | bytes 153604
  1379.5 16.2 %collective-permute-start.5 = (f32[400,32]{0,1:T(8,128)S(1)}, f32[400,32]{0,1:T(8,128)S(1)}, u32[]{:S(2)}, u32[]{:S(2)}) collective-permute-start(f32[400,32]{0,1:T(8,128)S(1)} %fusion), channel_id=1, source_target_pairs={{0,4},{1,5},{2,6},{3,7},{4,8},{5,9},{6,10},{7,11},{8,12},{9,13},{1... | collective-permute-start | bytes 153608
  1380.8 15.7 %copy-start.19 = (f32[400,32]{0,1:T(8,128)}, f32[400,32]{0,1:T(8,128)S(1)}, u32[]{:S(2)}) copy-start(f32[400,32]{0,1:T(8,128)S(1)} %collective-permute-done.23) | copy-start | bytes 153604
  1380.9 15.6 %collective-permute-start.6 = (f32[400,32]{0,1:T(8,128)S(1)}, f32[400,32]{0,1:T(8,128)S(1)}, u32[]{:S(2)}, u32[]{:S(2)}) collective-permute-start(f32[400,32]{0,1:T(8,128)S(1)} %fusion), channel_id=1, source_target_pairs={{0,5},{1,6},{2,7},{3,8},{4,9},{5,10},{6,11},{7,12},{8,13},{9,14},{... | collective-permute-start | bytes 153608
  1385.5 11.0 collective-permute-start.7
  1388.4 8.1 collective-permute-start.8
  1392.6 5.2 collective-permute-start.9
  1394.8 16.0 %copy-start.33 = (f32[29]{0:T(128)S(1)}, f32[29]{0:T(128)}, u32[]{:S(2)}) copy-start(f32[29]{0:T(128)} %param.18) | copy-start | bytes 352
  1394.8 16.5 %copy-start.12 = (f32[400,29]{0,1:T(8,128)S(1)}, f32[400,29]{0,1:T(8,128)}, u32[]{:S(2)}) copy-start(f32[400,29]{0,1:T(8,128)} %param.17) | copy-start | bytes 139204
  1395.8 19.6 %copy-start.32 = (f32[256]{0:T(256)S(1)}, f32[256]{0:T(256)}, u32[]{:S(2)}) copy-start(f32[256]{0:T(256)} %param.14) | copy-start | bytes 3076
  1395.8 17.5 %collective-permute-start = (f32[400,256]{0,1:T(8,128)}, f32[400,256]{0,1:T(8,128)S(1)}, u32[]{:S(2)}, u32[]{:S(2)}) collective-permute-start(f32[400,256]{0,1:T(8,128)} %divide_subtract_fusion), channel_id=1, source_target_pairs={{0,4},{4,8},{8,12},{12,16},{16,20},{20,24},{24,28},{28,32},{32,36}... | collective-permute-start | bytes 1228808 | tf_op jit(solution)/shard_map/ppermute | solution.py:13
  (8 other events, 5.4 us)
Sparse Core Ops, SparseCore 0:
  10.5 422.5 all-gather.2
  582.6 34.1 reduce-scatter.3
where the time goes:
time: 1430 us
  blocking collectives  727 us (51%)
  waiting for transfers between devices  409 us (29%)
  local copies, waits for them, and re-layouts  95.2 us (7%)
  other arithmetic  88.3 us (6%)
  starting transfers between devices  78.2 us (5%)
  between operations  15.4 us (1%)
    unnamed x1, blocking collectives  717 us
    all_gather x1, waiting for transfers between devices, shards(): lax.all_gather(relation_table.astype(jnp.bfloat16), ('blk', 'span'), axis...  399 us
    unnamed x24, starting transfers between devices  77.3 us
    unnamed x59, local copies, waits for them, and re-layouts  33.4 us
    scatter-add x2, other arithmetic, one_block(): relation_total = relation_total.at[:, relation_part].add(grad_relation)  29.7 us
  transfers between devices with their start and end apart: 28, of which 3 were waited for; matrix products, arithmetic and copies ran while one was open for 53% of the time, Pallas kernels for 0%

commit v1 on v0

v1 whole, which is shorter than its diff:
```python
import functools

import jax
import jax.numpy as jnp
from jax import lax
from jax.experimental import pallas as pl
from jax.experimental.pallas import tpu as pltpu
from jax.sharding import PartitionSpec as P

LEARN_RATE = 0.1
ADAGRAD_EPS = 1e-10
MESH = pl.DeviceIdType.MESH
LIVE = 1536
SHARE = 384
QROWS = 112
QPART = 50
QIM = 56
OWN_RELS = 29
VMEM = pl.BlockSpec(memory_space=pltpu.VMEM)
SMEM = pl.BlockSpec(memory_space=pltpu.SMEM)
NT = (((1,), (1,)), ((), ()))


def params(collective_id=None):
    if collective_id is None:
        return pltpu.CompilerParams(vmem_limit_bytes=56 * 2**20)
    return pltpu.CompilerParams(
        vmem_limit_bytes=56 * 2**20, collective_id=collective_id, has_side_effects=True
    )


def place():
    blk = lax.axis_index("blk")
    span = lax.axis_index("span")
    yh = lax.div(blk, 32)
    z = lax.rem(lax.div(blk, 4), 8)
    x = lax.rem(blk, 4)
    return yh, z, x, span


def device(yh, z, x, span):
    return (yh * 32 + lax.rem(z + 8, 8) * 4 + lax.rem(x + 4, 4), lax.rem(span, 4))


def remote(src, dst, send, recv, where):
    return pltpu.make_async_remote_copy(
        src_ref=src, dst_ref=dst, send_sem=send, recv_sem=recv, device_id=where, device_id_type=MESH
    )


def enter(peers):
    barrier = pltpu.get_barrier_semaphore()
    for peer in peers:
        pl.semaphore_signal(barrier, inc=1, device_id=peer, device_id_type=MESH)
    pl.semaphore_wait(barrier, len(peers))


def spread_kernel(
    piece_ref, low_ref, table_ref, low_all_ref, slots, p_send, p_recv, h_send, h_recv,
    y_send, y_recv, x_send, x_recv, r_send, r_recv, l_send, l_recv,
):
    yh, z, x, s = place()
    yo = 1 - yh
    span_peers = [device(yh, z, x, s + d) for d in (1, 2, 3)]
    x_peers = [device(yh, z, x + d, s) for d in (1, 2, 3)]
    y_peer = device(yo, z, x, s)
    right = device(yh, z + 1, x, s)
    left = device(yh, z - 1, x, s)
    enter(span_peers + x_peers + [y_peer, right, left])
    started = []

    def go(copy):
        copy.start()
        started.append(copy)
        return copy

    pieces = [
        go(remote(piece_ref.at[lax.rem(s + d, 4)], slots.at[d - 1], p_send.at[d - 1], p_recv.at[d - 1], span_peers[d - 1]))
        for d in (1, 2, 3)
    ]
    lows = [
        go(remote(low_ref, low_all_ref.at[s], h_send.at[d - 1], h_recv.at[d - 1], span_peers[d - 1]))
        for d in (1, 2, 3)
    ]
    low_all_ref[s] = low_ref[...]
    for copy in pieces:
        copy.wait_recv()
    table_ref[yh, z, x] = piece_ref[s] + slots[0] + slots[1] + slots[2]

    own = table_ref.at[yh, z, x]
    y_copy = go(remote(own, own, y_send, y_recv, y_peer))
    x_copies = [[], []]
    for d in (1, 2, 3):
        x_copies[0].append(go(remote(own, own, x_send.at[0, d - 1], x_recv.at[0, d - 1], x_peers[d - 1])))
    y_copy.wait_recv()
    other = table_ref.at[yo, z, x]
    for d in (1, 2, 3):
        x_copies[1].append(go(remote(other, other, x_send.at[1, d - 1], x_recv.at[1, d - 1], x_peers[d - 1])))

    def slab(chunk, zz):
        half = yh if chunk == 0 else yo
        return table_ref.at[half, lax.rem(zz + 8, 8)]

    steps = {("r", 0): 4, ("r", 1): 3, ("l", 0): 3, ("l", 1): 4}
    flying = {}
    for step in range(5):
        for chunk in (0, 1):
            if step == 0:
                for copy in x_copies[chunk]:
                    copy.wait_recv()
            for way in ("r", "l"):
                if 1 <= step <= steps[(way, chunk)]:
                    flying[(way, chunk, step - 1)].wait_recv()
                if step < steps[(way, chunk)]:
                    zz = z - step if way == "r" else z + step
                    send, recv = (r_send, r_recv) if way == "r" else (l_send, l_recv)
                    ref = slab(chunk, zz)
                    flying[(way, chunk, step)] = go(
                        remote(ref, ref, send.at[chunk, step], recv.at[chunk, step], right if way == "r" else left)
                    )
    for copy in lows:
        copy.wait_recv()
    for copy in started:
        copy.wait_send()


def spread(piece, low):
    dma = pltpu.SemaphoreType.DMA
    return pl.pallas_call(
        spread_kernel,
        out_shape=(
            jax.ShapeDtypeStruct((2, 8, 4, QROWS, 128), jnp.bfloat16),
            jax.ShapeDtypeStruct((4,) + low.shape, jnp.bfloat16),
        ),
        in_specs=[VMEM, VMEM],
        out_specs=(VMEM, VMEM),
        scratch_shapes=[
            pltpu.VMEM((3, QROWS, 128), jnp.bfloat16),
            dma((3,)), dma((3,)), dma((3,)), dma((3,)), dma, dma,
            dma((2, 3)), dma((2, 3)), dma((2, 4)), dma((2, 4)), dma((2, 4)), dma((2, 4)),
        ],
        compiler_params=params(0),
        name="spread",
    )(piece, low)


def one_hot(rows, index):
    row = lax.broadcasted_iota(jnp.int32, (rows, index.shape[1]), 0)
    return jnp.where(row == index, 1.0, 0.0).astype(jnp.bfloat16)


def pick_kernel(count_ref, index_ref, table_ref, slots_ref, picked_ref, low_hot, hot, total):
    at = lax.broadcasted_iota(jnp.int32, (8, LIVE), 1)
    kind = lax.broadcasted_iota(jnp.int32, (8, LIVE), 0)
    slots = jnp.full((8, LIVE), -1, jnp.int32)
    start = jnp.int32(0)
    for c in range(4):
        count = count_ref[c]
        listed = jnp.concatenate([index_ref[c], jnp.zeros((8, LIVE - 1024), jnp.int32)], axis=1)
        listed = pltpu.roll(listed, start, 1) + jnp.where(kind == 2, c * 256, 0)
        slots = jnp.where((at >= start) & (at < start + count), listed, slots)
        start = start + count
    slots = jnp.where(kind == 3, jnp.where(at < start, 1, 0), slots)
    slots_ref[...] = slots
    spot = slots[1:2]
    group = jnp.right_shift(spot, 7)
    low_hot[...] = one_hot(128, jnp.bitwise_and(spot, 127))
    total[...] = jnp.zeros_like(total)

    def chunk(i, carry):
        for k in range(8):
            mask = jnp.where(group == i * 8 + k, 1.0, 0.0).astype(jnp.bfloat16)
            hot[k * 128 : (k + 1) * 128, :] = low_hot[...] * mask
        block = jnp.concatenate([table_ref[i * 8 + k] for k in range(8)], axis=1)
        total[...] += jnp.dot(block, hot[...], preferred_element_type=jnp.float32)
        return carry

    lax.fori_loop(0, 8, chunk, 0)
    for c in range(4):
        picked_ref[c] = total[:, c * SHARE : (c + 1) * SHARE].astype(jnp.bfloat16)


def pick(counts, index, table):
    return pl.pallas_call(
        pick_kernel,
        out_shape=(
            jax.ShapeDtypeStruct((8, LIVE), jnp.int32),
            jax.ShapeDtypeStruct((4, QROWS, SHARE), jnp.bfloat16),
        ),
        in_specs=[SMEM, VMEM, VMEM],
        out_specs=(VMEM, VMEM),
        scratch_shapes=[
            pltpu.VMEM((128, LIVE), jnp.bfloat16),
            pltpu.VMEM((1024, LIVE), jnp.bfloat16),
            pltpu.VMEM((QROWS, LIVE), jnp.float32),
        ],
        compiler_params=params(),
        name="pick",
    )(counts, index, table)


def halves(value):
    high = value.astype(jnp.bfloat16)
    return high, (value - high.astype(jnp.float32)).astype(jnp.bfloat16)


def score_kernel(slots_ref, neg_ref, low_ref, rel_ref, rel_grad_ref, grads_ref):
    home = jnp.concatenate([low_ref[c, 0] for c in range(4)], axis=1)
    visit = jnp.concatenate([low_ref[c, 1] for c in range(4)], axis=1)
    live = slots_ref[3:4, :].astype(jnp.float32)
    hot_source = one_hot(1024, slots_ref[0:1, :])
    hot_dest = one_hot(1024, slots_ref[2:3, :])
    hot_neg = one_hot(1024, neg_ref[...])
    f32 = jnp.float32
    source = jnp.dot(home, hot_source, preferred_element_type=f32)
    dest = jnp.dot(visit, hot_dest, preferred_element_type=f32)
    negatives = jnp.dot(home, hot_neg, preferred_element_type=f32).astype(jnp.bfloat16)
    rel = [rel_ref[c].astype(f32) for c in range(4)]
    rel_re = jnp.concatenate([part[:QPART] for part in rel], axis=0)
    rel_im = jnp.concatenate([part[QIM : QIM + QPART] for part in rel], axis=0)
    middle = dest.shape[0] // 2
    dest_re, dest_im = dest[:middle], dest[middle:]
    trans = jnp.concatenate(
        [rel_re * dest_re - rel_im * dest_im, rel_re * dest_im + rel_im * dest_re], axis=0
    ).astype(jnp.bfloat16)
    positive = jnp.sum(source * trans.astype(f32), axis=0, keepdims=True)
    score = lax.dot_general(
        negatives, trans, (((0,), (0,)), ((), ())), preferred_element_type=f32
    )
    pos_weight = -live * jax.nn.sigmoid(-positive)
    weight = (live * jax.nn.sigmoid(score) * (1.0 / 1024.0)).astype(jnp.bfloat16)
    pull = jnp.dot(negatives, weight, preferred_element_type=f32)
    grad = pos_weight * source + pull
    grad_re, grad_im = grad[:middle], grad[middle:]
    out_re = dest_re * grad_re + dest_im * grad_im
    out_im = dest_re * grad_im - dest_im * grad_re
    pad = jnp.zeros((QIM - QPART, SHARE), f32)
    for c in range(4):
        rows = slice(c * QPART, (c + 1) * QPART)
        rel_grad_ref[c] = jnp.concatenate([out_re[rows], pad, out_im[rows], pad], axis=0)
    grad_dest = jnp.concatenate(
        [rel_re * grad_re + rel_im * grad_im, rel_re * grad_im - rel_im * grad_re], axis=0
    )
    share = jnp.dot(hot_neg, weight, preferred_element_type=f32) + pos_weight * hot_source.astype(f32)
    share_high, share_low = halves(share)
    dest_high, dest_low = halves(grad_dest)
    home_grad = lax.dot_general(trans, share_high, NT, preferred_element_type=f32) + lax.dot_general(
        trans, share_low, NT, preferred_element_type=f32
    )
    visit_grad = lax.dot_general(dest_high, hot_dest, NT, preferred_element_type=f32) + lax.dot_general(
        dest_low, hot_dest, NT, preferred_element_type=f32
    )
    for c in range(4):
        grads_ref[c, 0] = home_grad[:, c * 256 : (c + 1) * 256]
        grads_ref[c, 1] = visit_grad[:, c * 256 : (c + 1) * 256]


def score_slots(slots, neg_rows, low_all, rel):
    return pl.pallas_call(
        score_kernel,
        out_shape=(
            jax.ShapeDtypeStruct((4, QROWS, SHARE), jnp.float32),
            jax.ShapeDtypeStruct(low_all.shape, jnp.float32),
        ),
        in_specs=[VMEM] * 4,
        out_specs=(VMEM, VMEM),
        compiler_params=params(),
        name="score",
    )(slots, neg_rows, low_all, rel)


def put_kernel(slots_ref, grad_ref, out_ref, low_hot, hot, both):
    spot = slots_ref[1:2, :]
    group = jnp.right_shift(spot, 7)
    low_hot[...] = one_hot(128, jnp.bitwise_and(spot, 127))
    for c in range(4):
        high, low = halves(grad_ref[c])
        both[:QROWS, c * SHARE : (c + 1) * SHARE] = high
        both[QROWS:, c * SHARE : (c + 1) * SHARE] = low

    def chunk(i, carry):
        for k in range(8):
            mask = jnp.where(group == i * 8 + k, 1.0, 0.0).astype(jnp.bfloat16)
            hot[k * 128 : (k + 1) * 128, :] = low_hot[...] * mask
        sums = lax.dot_general(both[...], hot[...], NT, preferred_element_type=jnp.float32)
        sums = sums[:QROWS] + sums[QROWS:]
        for k in range(8):
            out_ref[i * 8 + k] = sums[:, k * 128 : (k + 1) * 128]
        return carry

    lax.fori_loop(0, 8, chunk, 0)


def put(slots, grad):
    return pl.pallas_call(
        put_kernel,
        out_shape=jax.ShapeDtypeStruct((64, QROWS, 128), jnp.float32),
        in_specs=[VMEM, VMEM],
        out_specs=VMEM,
        scratch_shapes=[
            pltpu.VMEM((128, LIVE), jnp.bfloat16),
            pltpu.VMEM((1024, LIVE), jnp.bfloat16),
            pltpu.VMEM((2 * QROWS, LIVE), jnp.bfloat16),
        ],
        compiler_params=params(),
        name="put",
    )(slots, grad)


def collect_kernel(
    rel_ref, grads_ref, rel_out_ref, grads_out_ref,
    r_buf, r_got, l_buf, l_got, total, x_got, x_sum, y_got, y_sum, m_got, o_buf, o_got,
    r_send, r_recv, l_send, l_recv, x_send, x_recv, y_send, y_recv, q_send, q_recv,
    m_send, m_recv, o_send, o_recv,
):
    yh, z, x, s = place()
    yo = 1 - yh
    span_peers = [device(yh, z, x, s + d) for d in (1, 2, 3)]
    x_peers = [device(yh, z, x + d, s) for d in (1, 2, 3)]
    y_peer = device(yo, z, x, s)
    right = device(yh, z + 1, x, s)
    left = device(yh, z - 1, x, s)
    mate_span = lax.div(s, 2) * 2 + 1 - lax.rem(s, 2)
    mate = device(yh, z, x, mate_span)
    across_span = lax.rem(s + 2, 4)
    across = device(yh, z, x, across_span)
    across_mate = lax.rem(mate_span + 2, 4)
    enter(span_peers + x_peers + [y_peer, right, left])
    started = []

    def go(copy):
        copy.start()
        started.append(copy)
        return copy

    far = {("r", 0): 4, ("r", 1): 3, ("l", 0): 3, ("l", 1): 4}
    flying = {}

    def ring(dist):
        for chunk in (0, 1):
            for way in ("r", "l"):
                if dist > far[(way, chunk)]:
                    continue
                buf, got, send, recv = (
                    (r_buf, r_got, r_send, r_recv) if way == "r" else (l_buf, l_got, l_send, l_recv)
                )
                zz = z + dist if way == "r" else z - dist
                value = rel_ref[chunk, lax.rem(zz + 8, 8)]
                if dist < far[(way, chunk)]:
                    flying[(way, chunk, dist + 1)].wait_recv()
                    value = value + got[chunk, dist].astype(jnp.float32)
                buf[chunk, dist - 1] = value.astype(jnp.bfloat16)
                flying[(way, chunk, dist)] = go(
                    remote(
                        buf.at[chunk, dist - 1], got.at[chunk, dist - 1],
                        send.at[chunk, dist - 1], recv.at[chunk, dist - 1],
                        right if way == "r" else left,
                    )
                )

    ring(4)
    m_copies = []
    for k in (1, 0):
        m_copies.append(go(remote(grads_ref.at[across_mate, k], m_got.at[1, k], m_send.at[1, k], m_recv.at[1, k], mate)))
    for k in (1, 0):
        m_copies.append(go(remote(grads_ref.at[mate_span, k], m_got.at[0, k], m_send.at[0, k], m_recv.at[0, k], mate)))
    ring(3)
    o_copies = []
    for i, k in enumerate((1, 0)):
        m_copies[i].wait_recv()
        o_buf[k] = grads_ref[across_span, k] + m_got[1, k]
        o_copies.append(go(remote(o_buf.at[k], o_got.at[k], o_send.at[k], o_recv.at[k], across)))
    ring(2)
    ring(1)
    x_copies = []
    for chunk in (0, 1):
        flying[("r", chunk, 1)].wait_recv()
        flying[("l", chunk, 1)].wait_recv()
        total[chunk] = (
            rel_ref[chunk, z] + r_got[chunk, 0].astype(jnp.float32) + l_got[chunk, 0].astype(jnp.float32)
        )
        for d in (1, 2, 3):
            x_copies.append(
                go(
                    remote(
                        total.at[chunk, lax.rem(x + d, 4)], x_got.at[chunk, d - 1],
                        x_send.at[chunk, d - 1], x_recv.at[chunk, d - 1], x_peers[d - 1],
                    )
                )
            )
    for copy in x_copies:
        copy.wait_recv()
    for chunk in (0, 1):
        x_sum[chunk] = total[chunk, x] + x_got[chunk, 0] + x_got[chunk, 1] + x_got[chunk, 2]
    y_copy = go(remote(x_sum.at[yo], y_got, y_send, y_recv, y_peer))
    y_copy.wait_recv()
    rel_out_ref[s] = x_sum[yh] + y_got[...]
    q_copies = [
        go(remote(rel_out_ref.at[s], rel_out_ref.at[s], q_send.at[d - 1], q_recv.at[d - 1], span_peers[d - 1]))
        for d in (1, 2, 3)
    ]
    for i, k in enumerate((1, 0)):
        m_copies[2 + i].wait_recv()
        o_copies[i].wait_recv()
        grads_out_ref[k] = grads_ref[s, k] + m_got[0, k] + o_got[k]
    for copy in q_copies:
        copy.wait_recv()
    for copy in started:
        copy.wait_send()


def collect(rel, grads):
    dma = pltpu.SemaphoreType.DMA
    f32, bf16 = jnp.float32, jnp.bfloat16
    pair = grads.shape[1:]
    return pl.pallas_call(
        collect_kernel,
        out_shape=(
            jax.ShapeDtypeStruct((4, QROWS, 128), f32),
            jax.ShapeDtypeStruct(pair, f32),
        ),
        in_specs=[VMEM, VMEM],
        out_specs=(VMEM, VMEM),
        scratch_shapes=[
            pltpu.VMEM((2, 4, 4, QROWS, 128), bf16), pltpu.VMEM((2, 4, 4, QROWS, 128), bf16),
            pltpu.VMEM((2, 4, 4, QROWS, 128), bf16), pltpu.VMEM((2, 4, 4, QROWS, 128), bf16),
            pltpu.VMEM((2, 4, QROWS, 128), f32), pltpu.VMEM((2, 3, QROWS, 128), f32),
            pltpu.VMEM((2, QROWS, 128), f32), pltpu.VMEM((QROWS, 128), f32), pltpu.VMEM((QROWS, 128), f32),
            pltpu.VMEM((2,) + pair, f32), pltpu.VMEM(pair, f32), pltpu.VMEM(pair, f32),
            dma((2, 4)), dma((2, 4)), dma((2, 4)), dma((2, 4)), dma((2, 3)), dma((2, 3)),
            dma, dma, dma((3,)), dma((3,)), dma((2, 2)), dma((2, 2)), dma((2,)), dma((2,)),
        ],
        compiler_params=params(1),
        name="collect",
    )(rel, grads)


def adagrad(table, state, grad_in):
    state_new = state + jnp.mean(grad_in * grad_in, axis=0)
    return (table - LEARN_RATE * grad_in / (jnp.sqrt(state_new)[None, :] + ADAGRAD_EPS), state_new)


def passed_along(value, axis, steps):
    count = lax.axis_size(axis)
    pairs = [(source, (source + steps) % count) for source in range(count)]
    return lax.ppermute(value, axis, pairs)


def shards(
    home_table, home_state, visit_table, visit_state, relation_table, relation_state,
    edge_src, edge_rel, edge_dst, edge_count, neg_rows,
):
    span = lax.axis_index("span")
    bf16 = jnp.bfloat16
    rel_spot = edge_rel[0, 0] // OWN_RELS * 32 + edge_rel[0, 0] % OWN_RELS
    index = jnp.stack(
        [edge_src[0, 0], rel_spot, edge_dst[0, 0], jnp.broadcast_to(edge_count[0, 0], rel_spot.shape)]
        + [jnp.zeros_like(rel_spot)] * 4
    )
    index = lax.all_gather(index, "span", axis=0)
    counts = index[:, 3, 0]
    quarters = relation_table.astype(bf16).reshape(2, 4, QPART, OWN_RELS).transpose(1, 0, 2, 3)
    quarters = jnp.pad(quarters, ((0, 0), (0, 0), (0, QIM - QPART), (0, 32 - OWN_RELS)))
    quarters = quarters.reshape(4, QROWS, 32)
    piece = lax.dynamic_update_slice(jnp.zeros((4, QROWS, 128), bf16), quarters, (0, 0, span * 32))
    low = jnp.stack([home_table, visit_table]).astype(bf16)
    table, low_all = spread(piece, low)
    slots, picked = pick(counts, index, table.reshape(64, QROWS, 128))
    rel = lax.all_to_all(picked, "span", 0, 0, tiled=True)
    own_slots = lax.dynamic_slice(slots, (0, span * SHARE), (8, SHARE))
    rel_grad, grads = score_slots(own_slots, neg_rows, low_all, rel)
    rel_grad = lax.all_to_all(rel_grad, "span", 0, 0, tiled=True)
    rel_all = put(slots, rel_grad).reshape(2, 8, 4, QROWS, 128)
    rel_sum, hv_sum = collect(rel_all, grads)
    visit_updated, visit_state_updated = adagrad(visit_table, visit_state, hv_sum[1])
    moved_table, moved_state = passed_along((visit_updated, visit_state_updated), "blk", 1)
    new_home, new_home_state = adagrad(home_table, home_state, hv_sum[0])
    own = lax.dynamic_slice(rel_sum, (0, 0, span * 32), (4, QROWS, 32))[:, :, :OWN_RELS]
    own = own.reshape(4, 2, QIM, OWN_RELS)[:, :, :QPART].transpose(1, 0, 2, 3)
    new_relation, new_relation_state = adagrad(
        relation_table, relation_state, own.reshape(8 * QPART, OWN_RELS)
    )
    return (new_home, new_home_state, moved_table, moved_state, new_relation, new_relation_state)


def solution(mesh):
    cols = P(None, ("blk", "span"))
    rows = P(("blk", "span"))
    slot = P("blk", "span", None)
    return jax.shard_map(
        shards,
        mesh=mesh,
        in_specs=(cols, rows, cols, rows, cols, rows, slot, slot, slot, P("blk", "span"), P("blk", None)),
        out_specs=(cols, rows, cols, rows, cols, rows),
        check_vma=False,
    )
```

time: 1430 us -> 191 us (0.13)
  blocking collectives: 727 us -> 23.6 us
  waiting for transfers between devices: 409 us -> 18.7 us
  Pallas kernels: 0 us -> 121 us
  local copies, waits for them, and re-layouts: 95.2 us -> 8.3 us
  other arithmetic: 88.3 us -> 8.61 us
  starting transfers between devices: 78.2 us -> 8.21 us
    unnamed x1 -> x0, blocking collectives: 717 us -> none
    all_gather x1 -> x0, waiting for transfers between devices: 399 us -> none  [shards(): lax.all_gather(relation_table.astype(jnp.bfloat16), ('blk', 'span'), axis...]
    pallas_call x0 -> x5, Pallas kernels: none -> 121 us  [the longest x1 51.3 us: spread(): pl.pallas_call(spread_kernel, out_shape=(jax.ShapeDtypeStruct((2, 8, 4, Q...]
    unnamed x24 -> x0, starting transfers between devices: 77.3 us -> none
    scatter-add x6 -> x0, other arithmetic: 55.4 us -> none  [the longest x2 29.7 us: one_block(): relation_total = relation_total.at[:, relation_part].add(grad_relation)]
    gather x10 -> x0, local copies, waits for them, and re-layouts: 34.9 us -> none  [the longest x4 17.5 us: one_block(): jnp.take(relation_all, relation_part, axis=1)]
    unnamed x59 -> x20, local copies, waits for them, and re-layouts: 33.4 us -> 2.71 us
    all_to_all x0 -> x1, blocking collectives: none -> 15.1 us  [shards(): rel_grad = lax.all_to_all(rel_grad, 'span', 0, 0, tiled=True)]
  transfers between devices with their start and end apart: 28 -> 3, of which waited for: 3 -> 3; matrix products, arithmetic and copies ran while one was open for 53% -> 3% of each run, Pallas kernels for 0% -> 0%
where the time goes in v1:
time: 191 us; the launch traced here: 190 us
  Pallas kernels  121 us (63%)
  blocking collectives  23.6 us (12%)
  waiting for transfers between devices  18.7 us (10%)
  other arithmetic  8.61 us (5%)
  local copies, waits for them, and re-layouts  8.3 us (4%)
  starting transfers between devices  8.21 us (4%)
    pallas_call x1, Pallas kernels, spread(): pl.pallas_call(spread_kernel, out_shape=(jax.ShapeDtypeStruct((2, 8, 4, Q...  51.3 us
    pallas_call x1, Pallas kernels, collect(): pl.pallas_call(collect_kernel, out_shape=(jax.ShapeDtypeStruct((4, QROWS,...  40.6 us
    all_to_all x1, blocking collectives, shards(): rel_grad = lax.all_to_all(rel_grad, 'span', 0, 0, tiled=True)  15.1 us
    ppermute x2, waiting for transfers between devices, passed_along(): return lax.ppermute(value, axis, pairs)  14 us
    pallas_call x1, Pallas kernels, put(): pl.pallas_call(put_kernel, out_shape=jax.ShapeDtypeStruct((64, QROWS, 128...  12.2 us
    pallas_call x1, Pallas kernels, score_slots(): pl.pallas_call(score_kernel, out_shape=(jax.ShapeDtypeStruct((4, QROWS, S...  9.33 us
    all_gather x1, blocking collectives, shards(): index = lax.all_gather(index, 'span', axis=0)  8.5 us
    pallas_call x1, Pallas kernels, pick(): pl.pallas_call(pick_kernel, out_shape=(jax.ShapeDtypeStruct((8, LIVE), jn...  7.64 us
  transfers between devices with their start and end apart: 3, of which 3 were waited for; matrix products, arithmetic and copies ran while one was open for 3% of the time, Pallas kernels for 0%

profile of v1, /device:TPU:1, one launch (start us, length us, event | category | flops | bytes accessed | tf_op | source)
XLA Modules:
  0.0 189.9 jit_solution(670599956884013131)
XLA Ops:
  1.3 0.7 fusion.3
  2.0 0.8 convert_element_type.6
  2.9 0.1 reshape.110
  3.0 0.2 copy.19
  3.2 0.7 stack.20
  3.9 8.5 %all-gather = s32[32,1024]{1,0:T(8,128)S(1)} all-gather(s32[8,1024]{1,0:T(8,128)S(1)} %stack.20), channel_id=2, replica_groups=mesh['blk'=64,'span'=4] {'span'}, dimensions={0}, use_global_device_ids=true | all-gather | bytes 163840 | tf_op jit(solution)/shard_map/all_gather | solution.py:460
  12.4 0.0 copy-start.3
  12.4 0.7 slice_reduce_fusion.count_ref
  13.1 1.2 convert_bitcast_fusion
  14.3 0.8 pad_maximum_fusion.low_ref
  15.1 1.1 dynamic_update_slice.3.piece_ref
  16.3 0.0 copy-start.4
  16.3 0.6 copy-done.4
  16.9 51.3 %spread.1 = (bf16[2,8,4,112,128]{4,3,2,1,0:T(8,128)(2,1)}, bf16[4,2,400,256]{3,2,1,0:T(8,128)(2,1)}) custom-call(bf16[4,112,128]{2,1,0:T(8,128)(2,1)} %copy-done.4, bf16[2,400,256]{2,1,0:T(8,128)(2,1)} %pad_maximum_fusion.low_ref), custom_call_target="tpu_custom_call" | custom-call | tf_op jit(solution)/shard_map/spread/pallas_call | solution.py:129
  68.2 0.0 copy-done.3
  68.2 7.6 %pick.1 = (s32[8,1536]{1,0:T(8,128)}, bf16[4,112,384]{2,1,0:T(8,128)(2,1)}) custom-call(s32[4]{0:T(128)} %slice_reduce_fusion.count_ref, s32[4,8,1024]{2,1,0:T(8,128)} %bitcast.47, bf16[64,112,128]{2,1,0:T(8,128)(2,1)} %bitcast.44), custom_call_target="tpu_custom_call" | custom-call | tf_op jit(solution)/shard_map/pick/pallas_call | solution.py:184
  75.8 6.9 %all-to-all-start = ((bf16[4,112,384]{2,1,0:T(8,128)(2,1)}), bf16[4,112,384]{2,1,0:T(8,128)(2,1)S(1)}, u32[]{:S(2)}, u32[]{:S(2)}) async-start(bf16[4,112,384]{2,1,0:T(8,128)(2,1)} %get-tuple-element.17), calls=%async_computation | async-start | bytes 688128 | tf_op jit(solution)/shard_map/all_to_all | solution.py:469
  82.7 1.3 constant_dynamic-slice_fusion.1.slots_ref
  84.0 4.7 %all-to-all-done.rel_ref = bf16[4,112,384]{2,1,0:T(8,128)(2,1)S(1)} async-done(((bf16[4,112,384]{2,1,0:T(8,128)(2,1)}), bf16[4,112,384]{2,1,0:T(8,128)(2,1)S(1)}, u32[]{:S(2)}, u32[]{:S(2)}) %all-to-all-start) | async-done | bytes 344096 | tf_op jit(solution)/shard_map/all_to_all | solution.py:469
  88.8 0.0 copy-start.2
  88.8 0.7 copy-done.2
  89.5 9.3 %score.1 = (f32[4,112,384]{2,1,0:T(8,128)}, f32[4,2,400,256]{3,2,1,0:T(8,128)}) custom-call(s32[8,384]{1,0:T(8,128)} %constant_dynamic-slice_fusion.1.slots_ref, s32[1,1024]{1,0:T(1,128)} %neg_ref.1, bf16[4,2,400,256]{3,2,1,0:T(8,128)(2,1)} %get-tuple-element.16.low_ref, bf16[4,112,384]{2,1,0:T(8,128)(2,1)} %copy-done.2), custom_call_target="tpu_custom_call" | custom-call | tf_op jit(solution)/shard_map/score/pallas_call | solution.py:259
  98.8 15.1 %all_to_all.10.grad_ref = f32[4,112,384]{2,1,0:T(8,128)} all-to-all(f32[4,112,384]{2,1,0:T(8,128)} %get-tuple-element.18), channel_id=1, replica_groups=mesh['blk'=64,'span'=4] {'span'}, dimensions={0} | all-to-all | bytes 1376256 | tf_op jit(solution)/shard_map/all_to_all | solution.py:472
  114.0 12.2 %put.1 = f32[64,112,128]{2,1,0:T(8,128)} custom-call(s32[8,1536]{1,0:T(8,128)} %get-tuple-element.15.slots_ref, f32[4,112,384]{2,1,0:T(8,128)} %all_to_all.10.grad_ref), custom_call_target="tpu_custom_call" | custom-call | tf_op jit(solution)/shard_map/put/pallas_call | solution.py:295
  126.2 0.0 copy-start.6
  126.2 0.0 copy-start.7
  126.2 0.0 copy-start
  126.2 0.0 copy-start.1
  126.2 40.6 %collect.1 = (f32[4,112,128]{2,1,0:T(8,128)}, f32[2,400,256]{2,1,0:T(8,128)}) custom-call(f32[2,8,4,112,128]{4,3,2,1,0:T(8,128)} %bitcast.43, f32[4,2,400,256]{3,2,1,0:T(8,128)} %get-tuple-element.19.grads_ref), custom_call_target="tpu_custom_call" | custom-call | tf_op jit(solution)/shard_map/collect/pallas_call | solution.py:416
  166.8 0.0 copy-start.8
  166.8 0.0 copy-start.5
  166.8 1.1 constant_dynamic-slice_fusion
  167.9 0.1 multiply_reduce_fusion.2
  168.0 1.2 multiply_reduce_fusion
  169.2 0.0 copy-done.6
  169.2 0.1 collective-permute-start.1
  169.3 0.2 copy.20
  169.5 0.1 mul.70
  169.6 0.0 copy-done.7
  169.6 0.6 sqrt_add_fusion.1
  170.2 0.0 copy-done
  170.2 0.0 copy-done.1
  170.2 2.0 %fusion = (f32[400,256]{1,0:T(8,128)S(1)}, f32[400,256]{1,0:T(8,128)}) fusion(f32[400,256]{1,0:T(8,128)S(1)} %copy-done, f32[2,400,256]{2,1,0:T(8,128)} %get-tuple-element.20, f32[256]{0:T(256)S(1)} %get-tuple-element.26, f32[400,256]{1,0:T(8,128)S(1)} %copy-done.1, f32[256]{0:T(256)S(1)} %get-tuple-element.28), kind=kLoop, calls=%fused_computation.2 | loop fusion | flops 614400 | bytes 2459648 | tf_op jit(solution)/shard_map/sub | solution.py:440
  172.2 1.3 collective-permute-start
  173.4 0.0 copy-done.8
  173.4 0.5 sqrt_add_fusion.2
  173.9 0.0 copy-done.5
  173.9 0.7 divide_subtract_fusion
  174.6 2.8 %collective-permute-done.1 = f32[256]{0:T(256)S(1)} collective-permute-done((f32[256]{0:T(256)S(1)}, f32[256]{0:T(256)S(1)}, u32[]{:S(2)}, u32[]{:S(2)}) %collective-permute-start.1) | collective-permute-done | bytes 1056 | tf_op jit(solution)/shard_map/ppermute | solution.py:446
  177.4 11.2 %collective-permute-done = f32[400,256]{1,0:T(8,128)S(1)} collective-permute-done((f32[400,256]{1,0:T(8,128)S(1)}, f32[400,256]{1,0:T(8,128)S(1)}, u32[]{:S(2)}, u32[]{:S(2)}) %collective-permute-start) | collective-permute-done | bytes 409632 | tf_op jit(solution)/shard_map/ppermute | solution.py:446
  188.6 0.8 copy.25
  189.4 0.6 copy.26
  (5 shorter events, 0.1 us)
Async XLA Ops:
  12.4 55.8 %copy-start.3 = (s32[32,1024]{1,0:T(8,128)}, s32[32,1024]{1,0:T(8,128)S(1)}, u32[]{:S(2)}) copy-start(s32[32,1024]{1,0:T(8,128)S(1)} %all-gather) | copy-start | bytes 393220
  16.3 0.6 copy-start.4
  75.8 12.9 %all-to-all-start = ((bf16[4,112,384]{2,1,0:T(8,128)(2,1)}), bf16[4,112,384]{2,1,0:T(8,128)(2,1)S(1)}, u32[]{:S(2)}, u32[]{:S(2)}) async-start(bf16[4,112,384]{2,1,0:T(8,128)(2,1)} %get-tuple-element.17), calls=%async_computation | async-start | bytes 688128 | tf_op jit(solution)/shard_map/all_to_all | solution.py:469
  88.8 0.7 copy-start.2
  126.2 43.0 %copy-start.6 = (f32[256]{0:T(256)S(1)}, f32[256]{0:T(256)}, u32[]{:S(2)}) copy-start(f32[256]{0:T(256)} %param.14) | copy-start | bytes 3076
  126.2 43.4 %copy-start.7 = (f32[256]{0:T(256)S(1)}, f32[256]{0:T(256)}, u32[]{:S(2)}) copy-start(f32[256]{0:T(256)} %param.12) | copy-start | bytes 3076
  126.2 44.0 %copy-start = (f32[400,256]{1,0:T(8,128)S(1)}, f32[400,256]{1,0:T(8,128)}, u32[]{:S(2)}) copy-start(f32[400,256]{1,0:T(8,128)} %param.13) | copy-start | bytes 1228804
  126.2 44.0 %copy-start.1 = (f32[400,256]{1,0:T(8,128)S(1)}, f32[400,256]{1,0:T(8,128)}, u32[]{:S(2)}) copy-start(f32[400,256]{1,0:T(8,128)} %param.11) | copy-start | bytes 1228804
  166.8 6.6 %copy-start.8 = (f32[29]{0:T(128)S(1)}, f32[29]{0:T(128)}, u32[]{:S(2)}) copy-start(f32[29]{0:T(128)} %param.16) | copy-start | bytes 352
  166.8 7.2 %copy-start.5 = (f32[400,29]{0,1:T(8,128)S(1)}, f32[400,29]{0,1:T(8,128)}, u32[]{:S(2)}) copy-start(f32[400,29]{0,1:T(8,128)} %param.15) | copy-start | bytes 139204
  169.2 8.2 %collective-permute-start.1 = (f32[256]{0:T(256)S(1)}, f32[256]{0:T(256)S(1)}, u32[]{:S(2)}, u32[]{:S(2)}) collective-permute-start(f32[256]{0:T(256)S(1)} %get-tuple-element.27), channel_id=1, source_target_pairs={{0,4},{4,8},{8,12},{12,16},{16,20},{20,24},{24,28},{28,32},{32,36}... | collective-permute-start | bytes 3080 | tf_op jit(solution)/shard_map/ppermute | solution.py:446
  172.2 16.5 %collective-permute-start = (f32[400,256]{1,0:T(8,128)S(1)}, f32[400,256]{1,0:T(8,128)S(1)}, u32[]{:S(2)}, u32[]{:S(2)}) collective-permute-start(f32[400,256]{1,0:T(8,128)S(1)} %get-tuple-element.30), channel_id=1, source_target_pairs={{0,4},{4,8},{8,12},{12,16},{16,20},{20,24},{24,28},{28,32},{32,36}... | collective-permute-start | bytes 1228808 | tf_op jit(solution)/shard_map/ppermute | solution.py:446

commit v2 on v1

v2 whole, which is shorter than its diff:
```python
import functools

import jax
import jax.numpy as jnp
from jax import lax
from jax.experimental import pallas as pl
from jax.experimental.pallas import tpu as pltpu
from jax.sharding import PartitionSpec as P

LEARN_RATE = 0.1
ADAGRAD_EPS = 1e-10
MESH = pl.DeviceIdType.MESH
LIVE = 1536
SHARE = 384
QROWS = 112
QPART = 50
QIM = 56
OWN_RELS = 29
VMEM = pl.BlockSpec(memory_space=pltpu.VMEM)
SMEM = pl.BlockSpec(memory_space=pltpu.SMEM)
NT = (((1,), (1,)), ((), ()))


def params(collective_id=None):
    if collective_id is None:
        return pltpu.CompilerParams(vmem_limit_bytes=56 * 2**20)
    return pltpu.CompilerParams(
        vmem_limit_bytes=56 * 2**20, collective_id=collective_id, has_side_effects=True
    )


def place():
    blk = lax.axis_index("blk")
    span = lax.axis_index("span")
    yh = lax.div(blk, 32)
    z = lax.rem(lax.div(blk, 4), 8)
    x = lax.rem(blk, 4)
    return yh, z, x, span


def device(yh, z, x, span):
    return (yh * 32 + lax.rem(z + 8, 8) * 4 + lax.rem(x + 4, 4), lax.rem(span, 4))


def remote(src, dst, send, recv, where):
    return pltpu.make_async_remote_copy(
        src_ref=src, dst_ref=dst, send_sem=send, recv_sem=recv, device_id=where, device_id_type=MESH
    )


def greet(peers):
    barrier = pltpu.get_barrier_semaphore()
    for peer in peers:
        pl.semaphore_signal(barrier, inc=1, device_id=peer, device_id_type=MESH)


def greeted(peers):
    pl.semaphore_wait(pltpu.get_barrier_semaphore(), len(peers))


def one_hot(rows, index):
    row = lax.broadcasted_iota(jnp.int32, (rows, index.shape[1]), 0)
    return jnp.where(row == index, 1.0, 0.0).astype(jnp.bfloat16)


def halves(value):
    high = value.astype(jnp.bfloat16)
    return high, (value - high.astype(jnp.float32)).astype(jnp.bfloat16)


def hot_lanes(low_hot, hot, group, first):
    for k in range(4):
        mask = jnp.where(group == first + k, 1.0, 0.0).astype(jnp.bfloat16)
        hot[k * 128 : (k + 1) * 128, :] = low_hot[...] * mask


FAR = {("r", 0): 4, ("r", 1): 3, ("l", 0): 3, ("l", 1): 4}


def gather_kernel(
    src_ref, spot_ref, dst_ref, count_ref, home_ref, visit_ref, relation_ref,
    slots_ref, low_all_ref, picked_ref,
    low, piece, got_piece, index, table, low_hot, hot, total, mine,
    i_send, i_recv, p_send, p_recv, h_send, h_recv, y_send, y_recv, x_send, x_recv,
    r_send, r_recv, l_send, l_recv, q_send, q_recv,
):
    f32, bf16 = jnp.float32, jnp.bfloat16
    yh, z, x, s = place()
    yo = 1 - yh
    span_peers = [device(yh, z, x, s + d) for d in (1, 2, 3)]
    x_peers = [device(yh, z, x + d, s) for d in (1, 2, 3)]
    y_peer = device(yo, z, x, s)
    right = device(yh, z + 1, x, s)
    left = device(yh, z - 1, x, s)
    peers = span_peers + x_peers + [y_peer, right, left]
    greet(peers)

    low[0] = home_ref[...].astype(bf16)
    low[1] = visit_ref[...].astype(bf16)
    low_all_ref[s] = low[...]
    index[s] = jnp.concatenate(
        [
            src_ref[...],
            spot_ref[...],
            dst_ref[...] + s * 256,
            jnp.broadcast_to(count_ref[...], (1, 1024)),
            jnp.zeros((4, 1024), jnp.int32),
        ],
        axis=0,
    )
    operators = relation_ref[...]
    middle = operators.shape[0] // 2
    for c in range(4):
        re = operators[c * QPART : (c + 1) * QPART]
        im = operators[middle + c * QPART : middle + (c + 1) * QPART]
        pad = jnp.zeros((QIM - QPART, OWN_RELS), f32)
        quarter = jnp.concatenate([re, pad, im, pad], axis=0)
        placed = jnp.zeros((QROWS, 128), f32)
        for k in range(4):
            parts = [quarter, jnp.zeros((QROWS, 128 - 32 * k - OWN_RELS), f32)]
            if k:
                parts = [jnp.zeros((QROWS, 32 * k), f32)] + parts
            placed = jnp.where(s == k, jnp.concatenate(parts, axis=1), placed)
        piece[c] = placed.astype(bf16)
    greeted(peers)
    started = []

    def go(copy):
        copy.start()
        started.append(copy)
        return copy

    pieces = [
        go(remote(piece.at[lax.rem(s + d, 4)], got_piece.at[d - 1], p_send.at[d - 1], p_recv.at[d - 1], span_peers[d - 1]))
        for d in (1, 2, 3)
    ]
    lists = [
        go(remote(index.at[s], index.at[s], i_send.at[d - 1], i_recv.at[d - 1], span_peers[d - 1]))
        for d in (1, 2, 3)
    ]
    for copy in pieces:
        copy.wait_recv()
    table[yh, z, x] = piece[s] + got_piece[0] + got_piece[1] + got_piece[2]

    own = table.at[yh, z, x]
    other = table.at[yo, z, x]
    y_copy = go(remote(own, own, y_send, y_recv, y_peer))
    x_copies = [[], []]
    for d in (1, 2, 3):
        x_copies[0].append(go(remote(own, own, x_send.at[0, d - 1], x_recv.at[0, d - 1], x_peers[d - 1])))
    for copy in lists:
        copy.wait_recv()
    y_copy.wait_recv()
    for d in (1, 2, 3):
        x_copies[1].append(go(remote(other, other, x_send.at[1, d - 1], x_recv.at[1, d - 1], x_peers[d - 1])))

    at = lax.broadcasted_iota(jnp.int32, (8, LIVE), 1)
    kind = lax.broadcasted_iota(jnp.int32, (8, LIVE), 0)
    slots = jnp.full((8, LIVE), -1, jnp.int32)
    start = jnp.zeros((1, 1), jnp.int32)
    for c in range(4):
        part = index[c]
        end = start + part[3:4, 0:1]
        listed = jnp.concatenate([part, jnp.zeros((8, LIVE - 1024), jnp.int32)], axis=1)
        if c:
            for bit in range(11):
                on = jnp.bitwise_and(jnp.right_shift(start, bit), 1) == 1
                listed = jnp.where(on, pltpu.roll(listed, 1 << bit, 1), listed)
        slots = jnp.where((at >= start) & (at < end), listed, slots)
        start = end
    slots = jnp.where(kind == 3, jnp.where(at < start, 1, 0), slots)
    slots_ref[...] = slots
    spot = slots[1:2]
    group = jnp.right_shift(spot, 7)
    low_hot[...] = one_hot(128, jnp.bitwise_and(spot, 127))
    total[...] = jnp.zeros_like(total)

    def half(chunk):
        return yh if chunk == 0 else yo

    def gather(chunk, zz):
        zz = lax.rem(zz + 8, 8)
        hot_lanes(low_hot, hot, group, half(chunk) * 32 + zz * 4)
        block = jnp.concatenate([table[half(chunk), zz, k] for k in range(4)], axis=1)
        total[...] += jnp.dot(block, hot[...], preferred_element_type=f32)

    flying = {}
    lows = []
    for step in range(5):
        for chunk in (0, 1):
            if step == 0:
                for copy in x_copies[chunk]:
                    copy.wait_recv()
            for way in ("r", "l"):
                if 1 <= step <= FAR[(way, chunk)]:
                    flying[(way, chunk, step - 1)].wait_recv()
                if step < FAR[(way, chunk)]:
                    zz = z - step if way == "r" else z + step
                    send, recv = (r_send, r_recv) if way == "r" else (l_send, l_recv)
                    ref = table.at[half(chunk), lax.rem(zz + 8, 8)]
                    flying[(way, chunk, step)] = go(
                        remote(ref, ref, send.at[chunk, step], recv.at[chunk, step], right if way == "r" else left)
                    )
            if step == 0:
                for d in (1, 2, 3):
                    lows.append(
                        go(
                            remote(
                                low.at[chunk], low_all_ref.at[s, chunk],
                                h_send.at[chunk, d - 1], h_recv.at[chunk, d - 1], span_peers[d - 1],
                            )
                        )
                    )
                gather(chunk, z)
            else:
                for way in ("r", "l"):
                    if step <= FAR[(way, chunk)]:
                        gather(chunk, z - step if way == "r" else z + step)
    for c in range(4):
        mine[c] = total[:, c * SHARE : (c + 1) * SHARE].astype(bf16)
    picks = [
        go(remote(mine.at[lax.rem(s + d, 4)], picked_ref.at[s], q_send.at[d - 1], q_recv.at[d - 1], span_peers[d - 1]))
        for d in (1, 2, 3)
    ]
    picked_ref[s] = mine[s]
    for copy in lows + picks:
        copy.wait_recv()
    for copy in started:
        copy.wait_send()


def gather_all(src, spot, dst, count, home, visit, relation):
    dma = pltpu.SemaphoreType.DMA
    bf16, f32, i32 = jnp.bfloat16, jnp.float32, jnp.int32
    pair = (2,) + home.shape
    quarters = (4, QROWS, SHARE)
    return pl.pallas_call(
        gather_kernel,
        out_shape=(
            jax.ShapeDtypeStruct((8, LIVE), i32),
            jax.ShapeDtypeStruct((4,) + pair, bf16),
            jax.ShapeDtypeStruct(quarters, bf16),
        ),
        in_specs=[VMEM] * 7,
        out_specs=(VMEM,) * 3,
        scratch_shapes=[
            pltpu.VMEM(pair, bf16), pltpu.VMEM((4, QROWS, 128), bf16), pltpu.VMEM((3, QROWS, 128), bf16),
            pltpu.VMEM((4, 8, 1024), i32), pltpu.VMEM((2, 8, 4, QROWS, 128), bf16),
            pltpu.VMEM((128, LIVE), bf16), pltpu.VMEM((512, LIVE), bf16), pltpu.VMEM((QROWS, LIVE), f32),
            pltpu.VMEM(quarters, bf16),
            dma((3,)), dma((3,)), dma((3,)), dma((3,)), dma((2, 3)), dma((2, 3)), dma, dma,
            dma((2, 3)), dma((2, 3)), dma((2, 4)), dma((2, 4)), dma((2, 4)), dma((2, 4)), dma((3,)), dma((3,)),
        ],
        compiler_params=params(0),
        name="gather",
    )(src, spot, dst, count, home, visit, relation)


def adagrad(table, state, grad_in):
    state_new = state + jnp.sum(grad_in * grad_in, axis=0, keepdims=True) * (1.0 / grad_in.shape[0])
    return table - LEARN_RATE * grad_in / (jnp.sqrt(state_new) + ADAGRAD_EPS), state_new


def update_kernel(
    slots_ref, neg_ref, low_ref, rel_ref, home_ref, home_state_ref, visit_ref, visit_state_ref,
    relation_ref, relation_state_ref,
    home_out, home_state_out, visit_out, visit_state_out, relation_out, relation_state_out,
    rel_grad, rel_got, both, low_hot, hot, grads,
    r_buf, r_got, l_buf, l_got, total, x_got, x_sum, y_got, q_got, m_got, o_buf, o_got, moved, moved_state,
    a_send, a_recv, r_send, r_recv, l_send, l_recv, x_send, x_recv, y_send, y_recv, q_send, q_recv,
    m_send, m_recv, o_send, o_recv, v_send, v_recv,
):
    f32, bf16 = jnp.float32, jnp.bfloat16
    yh, z, x, s = place()
    yo = 1 - yh
    blk = lax.axis_index("blk")
    span_peers = [device(yh, z, x, s + d) for d in (1, 2, 3)]
    x_peers = [device(yh, z, x + d, s) for d in (1, 2, 3)]
    y_peer = device(yo, z, x, s)
    right = device(yh, z + 1, x, s)
    left = device(yh, z - 1, x, s)
    after = (lax.rem(blk + 1, 64), s)
    before = (lax.rem(blk + 63, 64), s)
    mate_span = lax.div(s, 2) * 2 + 1 - lax.rem(s, 2)
    mate = device(yh, z, x, mate_span)
    across_span = lax.rem(s + 2, 4)
    across = device(yh, z, x, across_span)
    across_mate = lax.rem(mate_span + 2, 4)
    peers = span_peers + x_peers + [y_peer, right, left, after, before]
    greet(peers)
    started = []

    def go(copy):
        copy.start()
        started.append(copy)
        return copy

    mine = slots_ref[:, pl.ds(pl.multiple_of(s * SHARE, 128), SHARE)]
    home = jnp.concatenate([low_ref[c, 0] for c in range(4)], axis=1)
    visit = jnp.concatenate([low_ref[c, 1] for c in range(4)], axis=1)
    live = mine[3:4, :].astype(f32)
    hot_source = one_hot(1024, mine[0:1, :])
    hot_dest = one_hot(1024, mine[2:3, :])
    hot_neg = one_hot(1024, neg_ref[...])
    source = jnp.dot(home, hot_source, preferred_element_type=f32)
    dest = jnp.dot(visit, hot_dest, preferred_element_type=f32)
    negatives = jnp.dot(home, hot_neg, preferred_element_type=f32).astype(bf16)
    rel = [rel_ref[c].astype(f32) for c in range(4)]
    rel_re = jnp.concatenate([part[:QPART] for part in rel], axis=0)
    rel_im = jnp.concatenate([part[QIM : QIM + QPART] for part in rel], axis=0)
    middle = dest.shape[0] // 2
    dest_re, dest_im = dest[:middle], dest[middle:]
    trans = jnp.concatenate(
        [rel_re * dest_re - rel_im * dest_im, rel_re * dest_im + rel_im * dest_re], axis=0
    ).astype(bf16)
    positive = jnp.sum(source * trans.astype(f32), axis=0, keepdims=True)
    score = lax.dot_general(negatives, trans, (((0,), (0,)), ((), ())), preferred_element_type=f32)
    pos_weight = -live * jax.nn.sigmoid(-positive)
    weight = (live * jax.nn.sigmoid(score) * (1.0 / 1024.0)).astype(bf16)
    pull = jnp.dot(negatives, weight, preferred_element_type=f32)
    grad = pos_weight * source + pull
    grad_re, grad_im = grad[:middle], grad[middle:]
    out_re = dest_re * grad_re + dest_im * grad_im
    out_im = dest_re * grad_im - dest_im * grad_re
    pad = jnp.zeros((QIM - QPART, SHARE), f32)
    for c in range(4):
        rows = slice(c * QPART, (c + 1) * QPART)
        rel_grad[c] = jnp.concatenate([out_re[rows], pad, out_im[rows], pad], axis=0)
    greeted(peers)
    swaps = [
        go(remote(rel_grad.at[lax.rem(s + d, 4)], rel_got.at[s], a_send.at[d - 1], a_recv.at[d - 1], span_peers[d - 1]))
        for d in (1, 2, 3)
    ]
    rel_got[s] = rel_grad[s]
    grad_dest = jnp.concatenate(
        [rel_re * grad_re + rel_im * grad_im, rel_re * grad_im - rel_im * grad_re], axis=0
    )
    dest_high, dest_low = halves(grad_dest)
    visit_grad = lax.dot_general(dest_high, hot_dest, NT, preferred_element_type=f32) + lax.dot_general(
        dest_low, hot_dest, NT, preferred_element_type=f32
    )
    for c in range(4):
        grads[c, 1] = visit_grad[:, c * 256 : (c + 1) * 256]
    share = jnp.dot(hot_neg, weight, preferred_element_type=f32) + pos_weight * hot_source.astype(f32)
    share_high, share_low = halves(share)
    home_grad = lax.dot_general(trans, share_high, NT, preferred_element_type=f32) + lax.dot_general(
        trans, share_low, NT, preferred_element_type=f32
    )
    for c in range(4):
        grads[c, 0] = home_grad[:, c * 256 : (c + 1) * 256]

    spot = slots_ref[1:2, :]
    group = jnp.right_shift(spot, 7)
    low_hot[...] = one_hot(128, jnp.bitwise_and(spot, 127))
    for copy in swaps:
        copy.wait_recv()
    for c in range(4):
        high, low = halves(rel_got[c])
        both[:QROWS, c * SHARE : (c + 1) * SHARE] = high
        both[QROWS:, c * SHARE : (c + 1) * SHARE] = low

    def scatter(chunk, zz):
        hot_lanes(low_hot, hot, group, chunk * 32 + lax.rem(zz + 8, 8) * 4)
        sums = lax.dot_general(both[...], hot[...], NT, preferred_element_type=f32)
        sums = sums[:QROWS] + sums[QROWS:]
        return [sums[:, k * 128 : (k + 1) * 128] for k in range(4)]

    flying = {}

    def ring(dist):
        for chunk in (0, 1):
            for way in ("r", "l"):
                if dist > FAR[(way, chunk)]:
                    continue
                buf, got, send, recv = (
                    (r_buf, r_got, r_send, r_recv) if way == "r" else (l_buf, l_got, l_send, l_recv)
                )
                value = scatter(chunk, z + dist if way == "r" else z - dist)
                if dist < FAR[(way, chunk)]:
                    flying[(way, chunk, dist + 1)].wait_recv()
                    value = [v + got[chunk, dist, k].astype(f32) for k, v in enumerate(value)]
                for k in range(4):
                    buf[chunk, dist - 1, k] = value[k].astype(bf16)
                flying[(way, chunk, dist)] = go(
                    remote(
                        buf.at[chunk, dist - 1], got.at[chunk, dist - 1],
                        send.at[chunk, dist - 1], recv.at[chunk, dist - 1],
                        right if way == "r" else left,
                    )
                )

    ring(4)
    m_copies = {}
    for k in (1, 0):
        for i, row in ((1, across_mate), (0, mate_span)):
            m_copies[(i, k)] = go(remote(grads.at[row, k], m_got.at[i, k], m_send.at[i, k], m_recv.at[i, k], mate))
    ring(3)
    o_copies = {}

    def cross(k):
        m_copies[(1, k)].wait_recv()
        o_buf[k] = grads[across_span, k] + m_got[1, k]
        o_copies[k] = go(remote(o_buf.at[k], o_got.at[k], o_send.at[k], o_recv.at[k], across))

    def summed(k):
        m_copies[(0, k)].wait_recv()
        o_copies[k].wait_recv()
        return grads[s, k] + m_got[0, k] + o_got[k]

    cross(1)
    cross(0)
    ring(2)
    ring(1)
    table, state = adagrad(visit_ref[...], visit_state_ref[...], summed(1))
    moved[...] = table
    moved_state[...] = jnp.broadcast_to(state, moved_state.shape)
    moves = [
        go(remote(moved, visit_out, v_send.at[0], v_recv.at[0], after)),
        go(remote(moved_state, visit_state_out, v_send.at[1], v_recv.at[1], after)),
    ]
    x_copies = []
    for chunk in (0, 1):
        own = scatter(chunk, z)
        flying[("r", chunk, 1)].wait_recv()
        flying[("l", chunk, 1)].wait_recv()
        for k in range(4):
            total[chunk, k] = own[k] + r_got[chunk, 0, k].astype(f32) + l_got[chunk, 0, k].astype(f32)
        for d in (1, 2, 3):
            x_copies.append(
                go(
                    remote(
                        total.at[chunk, lax.rem(x + d, 4)], x_got.at[chunk, d - 1],
                        x_send.at[chunk, d - 1], x_recv.at[chunk, d - 1], x_peers[d - 1],
                    )
                )
            )
    for copy in x_copies:
        copy.wait_recv()
    for chunk in (0, 1):
        x_sum[chunk] = total[chunk, x] + x_got[chunk, 0] + x_got[chunk, 1] + x_got[chunk, 2]
    y_copy = go(remote(x_sum.at[yo], y_got, y_send, y_recv, y_peer))
    home_new, home_state_new = adagrad(home_ref[...], home_state_ref[...], summed(0))
    home_out[...] = home_new
    home_state_out[...] = home_state_new
    y_copy.wait_recv()
    q_got[s] = x_sum[yh] + y_got[...]
    quarters = [
        go(remote(q_got.at[s], q_got.at[s], q_send.at[d - 1], q_recv.at[d - 1], span_peers[d - 1]))
        for d in (1, 2, 3)
    ]
    for copy in quarters:
        copy.wait_recv()
    res, ims = [], []
    for c in range(4):
        part = q_got[c]
        own = jnp.zeros((QROWS, OWN_RELS), f32)
        for k in range(4):
            own = jnp.where(s == k, part[:, 32 * k : 32 * k + OWN_RELS], own)
        res.append(own[:QPART])
        ims.append(own[QIM : QIM + QPART])
    table, state = adagrad(relation_ref[...], relation_state_ref[...], jnp.concatenate(res + ims, axis=0))
    relation_out[...] = table
    relation_state_out[...] = state
    for copy in moves:
        copy.wait_recv()
    for copy in started:
        copy.wait_send()


def update_all(slots, neg_rows, low_all, rel, home, home_state, visit, visit_state, relation, relation_state):
    dma = pltpu.SemaphoreType.DMA
    f32, bf16 = jnp.float32, jnp.bfloat16
    pair = (2,) + home.shape
    ring = pltpu.VMEM((2, 4, 4, QROWS, 128), bf16)
    return pl.pallas_call(
        update_kernel,
        out_shape=(
            jax.ShapeDtypeStruct(home.shape, f32),
            jax.ShapeDtypeStruct(home_state.shape, f32),
            jax.ShapeDtypeStruct(visit.shape, f32),
            jax.ShapeDtypeStruct((8, visit.shape[1]), f32),
            jax.ShapeDtypeStruct(relation.shape, f32),
            jax.ShapeDtypeStruct(relation_state.shape, f32),
        ),
        in_specs=[VMEM] * 10,
        out_specs=(VMEM,) * 6,
        scratch_shapes=[
            pltpu.VMEM((4, QROWS, SHARE), f32), pltpu.VMEM((4, QROWS, SHARE), f32),
            pltpu.VMEM((2 * QROWS, LIVE), bf16), pltpu.VMEM((128, LIVE), bf16), pltpu.VMEM((512, LIVE), bf16),
            pltpu.VMEM((4,) + pair, f32),
            ring, ring, ring, ring,
            pltpu.VMEM((2, 4, QROWS, 128), f32), pltpu.VMEM((2, 3, QROWS, 128), f32),
            pltpu.VMEM((2, QROWS, 128), f32), pltpu.VMEM((QROWS, 128), f32), pltpu.VMEM((4, QROWS, 128), f32),
            pltpu.VMEM((2,) + pair, f32), pltpu.VMEM(pair, f32), pltpu.VMEM(pair, f32),
            pltpu.VMEM(visit.shape, f32), pltpu.VMEM((8, visit.shape[1]), f32),
            dma((3,)), dma((3,)), dma((2, 4)), dma((2, 4)), dma((2, 4)), dma((2, 4)), dma((2, 3)), dma((2, 3)),
            dma, dma, dma((3,)), dma((3,)), dma((2, 2)), dma((2, 2)), dma((2,)), dma((2,)), dma((2,)), dma((2,)),
        ],
        compiler_params=params(1),
        name="update",
    )(slots, neg_rows, low_all, rel, home, home_state, visit, visit_state, relation, relation_state)


def shards(
    home_table, home_state, visit_table, visit_state, relation_table, relation_state,
    edge_src, edge_rel, edge_dst, edge_count, neg_rows,
):
    spot = edge_rel[0] // OWN_RELS * 32 + edge_rel[0] % OWN_RELS
    slots, low_all, rel = gather_all(
        edge_src[0], spot, edge_dst[0], edge_count, home_table, visit_table, relation_table
    )
    new_home, new_home_state, moved, moved_state, new_relation, new_relation_state = update_all(
        slots, neg_rows, low_all, rel, home_table, home_state[None], visit_table, visit_state[None],
        relation_table, relation_state[None],
    )
    return (new_home, new_home_state[0], moved, moved_state[0], new_relation, new_relation_state[0])


def solution(mesh):
    cols = P(None, ("blk", "span"))
    rows = P(("blk", "span"))
    slot = P("blk", "span", None)
    return jax.shard_map(
        shards,
        mesh=mesh,
        in_specs=(cols, rows, cols, rows, cols, rows, slot, slot, slot, P("blk", "span"), P("blk", None)),
        out_specs=(cols, rows, cols, rows, cols, rows),
        check_vma=False,
    )
```

time: 191 us -> 117 us (0.61)
  blocking collectives: 23.6 us -> 0 us
  waiting for transfers between devices: 18.7 us -> 0 us
  Pallas kernels: 121 us -> 103 us
  starting transfers between devices: 8.21 us -> 0 us
  other arithmetic: 8.61 us -> 1.32 us
    pallas_call x5 -> x2, Pallas kernels: 121 us -> 103 us  [the longest x1 57.7 us: update_all(): pl.pallas_call(update_kernel, out_shape=(jax.ShapeDtypeStruct(home.shape,...]
    all_to_all x1 -> x0, blocking collectives: 15.1 us -> none  [shards(): rel_grad = lax.all_to_all(rel_grad, 'span', 0, 0, tiled=True)]
    ppermute x2 -> x0, waiting for transfers between devices: 14 us -> none  [passed_along(): return lax.ppermute(value, axis, pairs)]
    all_gather x1 -> x0, blocking collectives: 8.5 us -> none  [shards(): index = lax.all_gather(index, 'span', axis=0)]
    all_to_all x1 -> x0, starting transfers between devices: 6.87 us -> none  [shards(): rel = lax.all_to_all(picked, 'span', 0, 0, tiled=True)]
    unnamed x20 -> x8, local copies, waits for them, and re-layouts: 2.71 us -> 8.64 us
    all_to_all x1 -> x0, waiting for transfers between devices: 4.74 us -> none  [shards(): rel = lax.all_to_all(picked, 'span', 0, 0, tiled=True)]
    sub x2 -> x0, other arithmetic: 2.7 us -> none  [adagrad(): table - LEARN_RATE * grad_in / (jnp.sqrt(state_new)[None, :] + ADAGRAD_EPS)]
  transfers between devices with their start and end apart: 3 -> 0, of which waited for: 3 -> 0; matrix products, arithmetic and copies ran while one was open for 3% -> 0% of each run, Pallas kernels for 0% -> 0%
where the time goes in v2:
time: 117 us; the launch traced here: 116 us
  Pallas kernels  103 us (88%)
  local copies, waits for them, and re-layouts  9.9 us (8%)
  other arithmetic  1.32 us (1%)
  between operations  1.31 us (1%)
    pallas_call x1, Pallas kernels, update_all(): pl.pallas_call(update_kernel, out_shape=(jax.ShapeDtypeStruct(home.shape,...  57.7 us
    pallas_call x1, Pallas kernels, gather_all(): pl.pallas_call(gather_kernel, out_shape=(jax.ShapeDtypeStruct((8, LIVE),...  45.6 us
    unnamed x8, local copies, waits for them, and re-layouts  8.64 us

profile of v2, /device:TPU:1, one launch (start us, length us, event | category | flops | bytes accessed | tf_op | source)
XLA Modules:
  0.0 115.8 jit_solution(693431374700439129)
XLA Ops:
  1.3 1.3 %fusion.1.spot_ref = s32[1,1024]{1,0:T(1,128)} fusion(s32[1,1,1024]{2,1,0:T(1,128)} %param.18), kind=kLoop, calls=%fused_computation.3 | loop fusion | flops 14336 | bytes 8192 | tf_op jit(solution)/shard_map/add | solution.py:508
  2.6 1.7 %copy.17.relation_ref = f32[400,29]{1,0:T(8,128)} copy(f32[400,29]{0,1:T(8,128)} %param.15) | data formatting | bytes 92800 | tf_op args[4]
  4.3 45.6 %gather.1 = (s32[8,1536]{1,0:T(8,128)}, bf16[4,2,400,256]{3,2,1,0:T(8,128)(2,1)}, bf16[4,112,384]{2,1,0:T(8,128)(2,1)}) custom-call(s32[1,1024]{1,0:T(1,128)} %bitcast.23, s32[1,1024]{1,0:T(1,128)} %fusion.1.spot_ref, s32[1,1024]{1,0:T(1,128)} %bitcast.24, s32[1,1]{1,0:T(1,128)S(6)} %copy.24.count_ref, f32[400,256]{1,0:T(8,128)} %home_ref.3, ...), custom_call_target="tpu_custom_call" | custom-call | tf_op jit(solution)/shard_map/gather/pallas_call | solution.py:237
  49.8 57.7 %update.1 = (f32[400,256]{1,0:T(8,128)}, f32[1,256]{1,0:T(1,128)}, f32[400,256]{1,0:T(8,128)}, f32[8,256]{1,0:T(8,128)}, f32[400,29]{1,0:T(8,128)}, /*index=5*/f32[1,29]{1,0:T(1,128)}) custom-call(s32[8,1536]{1,0:T(8,128)} %get-tuple-element.15.slots_ref, s32[1,1024]{1,0:T(1,128)} %neg_ref.1, bf16[4,2,400,256]{3,2,1,0:T(8,128)(2,1)} %get-tuple-element.16.low_ref, ...), custom_call_target="tpu_custom_call" | custom-call | tf_op jit(solution)/shard_map/update/pallas_call | solution.py:475
  107.5 0.0 copy-start
  107.5 1.3 %slice.3 = f32[1,256]{1,0:T(1,128)} slice(f32[8,256]{1,0:T(8,128)} %get-tuple-element.21), slice={[0:1], [0:256]} | slice | bytes 2048 | tf_op jit(solution)/shard_map/slice | solution.py:516
  108.8 1.7 %copy.19 = f32[400,29]{0,1:T(8,128)} copy(f32[400,29]{1,0:T(8,128)} %get-tuple-element.28) | data formatting | bytes 92800
  110.5 1.8 %copy.25 = f32[400,256]{1,0:T(8,128)} copy(f32[400,256]{1,0:T(8,128)} %get-tuple-element.36) | data formatting | bytes 819200
  112.2 1.2 %copy.26 = f32[256]{0:T(256)} copy(f32[256]{0:T(256)} %bitcast.28) | data formatting | bytes 2048
  113.5 1.8 %copy.27 = f32[400,256]{1,0:T(8,128)} copy(f32[400,256]{1,0:T(8,128)} %get-tuple-element.38) | data formatting | bytes 819200
  115.2 0.0 copy-done
  115.2 0.5 copy.28
Async XLA Ops:
  107.5 7.7 %copy-start = (f32[1,29]{1,0:T(1,128)S(1)}, f32[1,29]{1,0:T(1,128)}, u32[]{:S(2)}) copy-start(f32[1,29]{1,0:T(1,128)} %get-tuple-element.23) | copy-start | bytes 352

commit v3 on v2

v3 whole, which is shorter than its diff:
```python
import functools

import jax
import jax.numpy as jnp
from jax import lax
from jax.experimental import pallas as pl
from jax.experimental.pallas import tpu as pltpu
from jax.sharding import PartitionSpec as P

LEARN_RATE = 0.1
ADAGRAD_EPS = 1e-10
MESH = pl.DeviceIdType.MESH
LIVE = 1536
SHARE = 384
QROWS = 112
QPART = 50
QIM = 56
OWN_RELS = 29
VMEM = pl.BlockSpec(memory_space=pltpu.VMEM)
SMEM = pl.BlockSpec(memory_space=pltpu.SMEM)
NT = (((1,), (1,)), ((), ()))


def params(collective_id=None):
    if collective_id is None:
        return pltpu.CompilerParams(vmem_limit_bytes=56 * 2**20)
    return pltpu.CompilerParams(
        vmem_limit_bytes=56 * 2**20, collective_id=collective_id, has_side_effects=True
    )


def place():
    blk = lax.axis_index("blk")
    span = lax.axis_index("span")
    yh = lax.div(blk, 32)
    z = lax.rem(lax.div(blk, 4), 8)
    x = lax.rem(blk, 4)
    return yh, z, x, span


def device(yh, z, x, span):
    return (yh * 32 + lax.rem(z + 8, 8) * 4 + lax.rem(x + 4, 4), lax.rem(span, 4))


def remote(src, dst, send, recv, where):
    return pltpu.make_async_remote_copy(
        src_ref=src, dst_ref=dst, send_sem=send, recv_sem=recv, device_id=where, device_id_type=MESH
    )


def greet(peers):
    barrier = pltpu.get_barrier_semaphore()
    for peer in peers:
        pl.semaphore_signal(barrier, inc=1, device_id=peer, device_id_type=MESH)


def greeted(peers):
    pl.semaphore_wait(pltpu.get_barrier_semaphore(), len(peers))


def one_hot(rows, index):
    row = lax.broadcasted_iota(jnp.int32, (rows, index.shape[1]), 0)
    return jnp.where(row == index, 1.0, 0.0).astype(jnp.bfloat16)


def halves(value):
    high = value.astype(jnp.bfloat16)
    return high, (value - high.astype(jnp.float32)).astype(jnp.bfloat16)


def hot_lanes(low_hot, hot, group, first):
    for k in range(4):
        mask = jnp.where(group == first + k, 1.0, 0.0).astype(jnp.bfloat16)
        hot[k * 128 : (k + 1) * 128, :] = low_hot[...] * mask


FAR = {("r", 0): 4, ("r", 1): 3, ("l", 0): 3, ("l", 1): 4}


def round_kernel(
    src_ref, rel_ref, dst_ref, count_ref, neg_ref, home_ref, visit_ref, visit_state_ref, relation_ref,
    home_grad_ref, visit_out, visit_state_out, visit_grad_ref, quarter_ref,
    low, low_all, piece, got_piece, index, table, low_hot, hot, total, mine, picked,
    hot_neg, negatives, rel_grad, rel_got, both, grads,
    r_buf, r_got, l_buf, l_got, row_sum, x_got, x_sum, y_got, m_got, o_buf, o_got, visit_sum,
    i_send, i_recv, p_send, p_recv, h_send, h_recv, y_send, y_recv, x_send, x_recv,
    r_send, r_recv, l_send, l_recv, k_send, k_recv, v_send, v_recv, a_send, a_recv,
    rr_send, rr_recv, ll_send, ll_recv, xx_send, xx_recv, yy_send, yy_recv, q_send, q_recv,
    m_send, m_recv, o_send, o_recv,
):
    f32, bf16 = jnp.float32, jnp.bfloat16
    yh, z, x, s = place()
    yo = 1 - yh
    blk = lax.axis_index("blk")
    span_peers = [device(yh, z, x, s + d) for d in (1, 2, 3)]
    x_peers = [device(yh, z, x + d, s) for d in (1, 2, 3)]
    y_peer = device(yo, z, x, s)
    right = device(yh, z + 1, x, s)
    left = device(yh, z - 1, x, s)
    after = (lax.rem(blk + 1, 64), s)
    before = (lax.rem(blk + 63, 64), s)
    mate_span = lax.div(s, 2) * 2 + 1 - lax.rem(s, 2)
    mate = device(yh, z, x, mate_span)
    across_span = lax.rem(s + 2, 4)
    across = device(yh, z, x, across_span)
    across_mate = lax.rem(mate_span + 2, 4)
    peers = span_peers + x_peers + [y_peer, right, left, after, before]
    greet(peers)

    operators = jnp.concatenate([relation_ref[...], jnp.zeros((32 - OWN_RELS, 8 * QPART), f32)], axis=0).T
    middle = operators.shape[0] // 2
    pad = jnp.zeros((QIM - QPART, 32), f32)
    for c in range(4):
        re = operators[c * QPART : (c + 1) * QPART]
        im = operators[middle + c * QPART : middle + (c + 1) * QPART]
        quarter = jnp.concatenate([re, pad, im, pad], axis=0)
        placed = jnp.zeros((QROWS, 128), f32)
        for k in range(4):
            parts = [jnp.zeros((QROWS, 32), f32)] * 4
            parts[k] = quarter
            placed = jnp.where(s == k, jnp.concatenate(parts, axis=1), placed)
        piece[c] = placed.astype(bf16)
    rel = rel_ref[...]
    owner = jnp.right_shift(rel * 4520, 17)
    index[s] = jnp.concatenate(
        [
            src_ref[...],
            rel + owner * (32 - OWN_RELS),
            dst_ref[...] + s * 256,
            jnp.broadcast_to(count_ref[...], (1, 1024)),
            jnp.zeros((4, 1024), jnp.int32),
        ],
        axis=0,
    )
    low[0] = home_ref[...].astype(bf16)
    low[1] = visit_ref[...].astype(bf16)
    low_all[s] = low[...]
    greeted(peers)
    started = []

    def go(copy):
        copy.start()
        started.append(copy)
        return copy

    def to_span(src_of, dst, send, recv):
        return [
            go(remote(src_of(lax.rem(s + d, 4)), dst, send.at[d - 1], recv.at[d - 1], span_peers[d - 1]))
            for d in (1, 2, 3)
        ]

    pieces = [
        go(remote(piece.at[lax.rem(s + d, 4)], got_piece.at[d - 1], p_send.at[d - 1], p_recv.at[d - 1], span_peers[d - 1]))
        for d in (1, 2, 3)
    ]
    lists = to_span(lambda peer: index.at[s], index.at[s], i_send, i_recv)
    for copy in pieces:
        copy.wait_recv()
    table[yh, z, x] = piece[s] + got_piece[0] + got_piece[1] + got_piece[2]

    own = table.at[yh, z, x]
    other = table.at[yo, z, x]
    y_copy = go(remote(own, own, y_send, y_recv, y_peer))
    x_copies = [[], []]
    for d in (1, 2, 3):
        x_copies[0].append(go(remote(own, own, x_send.at[0, d - 1], x_recv.at[0, d - 1], x_peers[d - 1])))
    for copy in lists:
        copy.wait_recv()
    y_copy.wait_recv()
    for d in (1, 2, 3):
        x_copies[1].append(go(remote(other, other, x_send.at[1, d - 1], x_recv.at[1, d - 1], x_peers[d - 1])))

    at = lax.broadcasted_iota(jnp.int32, (8, LIVE), 1)
    kind = lax.broadcasted_iota(jnp.int32, (8, LIVE), 0)
    slots = jnp.full((8, LIVE), -1, jnp.int32)
    start = jnp.zeros((1, 1), jnp.int32)
    for c in range(4):
        part = index[c]
        end = start + part[3:4, 0:1]
        listed = jnp.concatenate([part, jnp.zeros((8, LIVE - 1024), jnp.int32)], axis=1)
        if c:
            for bit in range(11):
                on = jnp.bitwise_and(jnp.right_shift(start, bit), 1) == 1
                listed = jnp.where(on, pltpu.roll(listed, 1 << bit, 1), listed)
        slots = jnp.where((at >= start) & (at < end), listed, slots)
        start = end
    slots = jnp.where(kind == 3, jnp.where(at < start, 1, 0), slots)
    share_slots = jnp.zeros((8, SHARE), jnp.int32)
    for c in range(4):
        share_slots = jnp.where(s == c, slots[:, c * SHARE : (c + 1) * SHARE], share_slots)
    spot = slots[1:2]
    group = jnp.right_shift(spot, 7)
    low_hot[...] = one_hot(128, jnp.bitwise_and(spot, 127))
    total[...] = jnp.zeros_like(total)

    def half(chunk):
        return yh if chunk == 0 else yo

    def gather(chunk, zz):
        zz = lax.rem(zz + 8, 8)
        hot_lanes(low_hot, hot, group, half(chunk) * 32 + zz * 4)
        block = jnp.concatenate([table[half(chunk), zz, k] for k in range(4)], axis=1)
        total[...] += jnp.dot(block, hot[...], preferred_element_type=f32)

    flying = {}
    lows = [[], []]
    for step in range(5):
        for chunk in (0, 1):
            if step == 0:
                for copy in x_copies[chunk]:
                    copy.wait_recv()
            for way in ("r", "l"):
                if 1 <= step <= FAR[(way, chunk)]:
                    flying[(way, chunk, step - 1)].wait_recv()
                if step < FAR[(way, chunk)]:
                    zz = z - step if way == "r" else z + step
                    send, recv = (r_send, r_recv) if way == "r" else (l_send, l_recv)
                    ref = table.at[half(chunk), lax.rem(zz + 8, 8)]
                    flying[(way, chunk, step)] = go(
                        remote(ref, ref, send.at[chunk, step], recv.at[chunk, step], right if way == "r" else left)
                    )
            if step == 0:
                lows[chunk] = to_span(lambda peer: low.at[chunk], low_all.at[s, chunk], h_send.at[chunk], h_recv.at[chunk])
                gather(chunk, z)
            else:
                for way in ("r", "l"):
                    if step <= FAR[(way, chunk)]:
                        gather(chunk, z - step if way == "r" else z + step)
            if step == 3 and chunk == 0:
                for copy in lows[0]:
                    copy.wait_recv()
                hot_neg[...] = one_hot(1024, neg_ref[...])
            if step == 3 and chunk == 1:
                home = jnp.concatenate([low_all[c, 0] for c in range(4)], axis=1)
                negatives[...] = jnp.dot(home, hot_neg[...], preferred_element_type=f32).astype(bf16)
    for c in range(4):
        mine[c] = total[:, c * SHARE : (c + 1) * SHARE].astype(bf16)
    picks = to_span(lambda peer: mine.at[peer], picked.at[s], k_send, k_recv)
    picked[s] = mine[s]
    moves = [
        go(remote(visit_ref, visit_out, v_send.at[0], v_recv.at[0], after)),
        go(remote(visit_state_ref, visit_state_out, v_send.at[1], v_recv.at[1], after)),
    ]

    for copy in lows[1]:
        copy.wait_recv()
    visit = jnp.concatenate([low_all[c, 1] for c in range(4)], axis=1)
    live = share_slots[3:4, :].astype(f32)
    hot_source = one_hot(1024, share_slots[0:1, :])
    hot_dest = one_hot(1024, share_slots[2:3, :])
    source = jnp.dot(home, hot_source, preferred_element_type=f32)
    dest = jnp.dot(visit, hot_dest, preferred_element_type=f32)
    dest_re, dest_im = dest[:middle], dest[middle:]
    for copy in picks:
        copy.wait_recv()
    rel = [picked[c].astype(f32) for c in range(4)]
    rel_re = jnp.concatenate([part[:QPART] for part in rel], axis=0)
    rel_im = jnp.concatenate([part[QIM : QIM + QPART] for part in rel], axis=0)
    trans = jnp.concatenate(
        [rel_re * dest_re - rel_im * dest_im, rel_re * dest_im + rel_im * dest_re], axis=0
    ).astype(bf16)
    positive = jnp.sum(source * trans.astype(f32), axis=0, keepdims=True)
    score = lax.dot_general(negatives[...], trans, (((0,), (0,)), ((), ())), preferred_element_type=f32)
    pos_weight = -live * jax.nn.sigmoid(-positive)
    weight = (live * jax.nn.sigmoid(score) * (1.0 / 1024.0)).astype(bf16)
    pull = jnp.dot(negatives[...], weight, preferred_element_type=f32)
    grad = pos_weight * source + pull
    grad_re, grad_im = grad[:middle], grad[middle:]
    out_re = dest_re * grad_re + dest_im * grad_im
    out_im = dest_re * grad_im - dest_im * grad_re
    pad = jnp.zeros((QIM - QPART, SHARE), f32)
    for c in range(4):
        rows = slice(c * QPART, (c + 1) * QPART)
        rel_grad[c] = jnp.concatenate([out_re[rows], pad, out_im[rows], pad], axis=0)
    swaps = to_span(lambda peer: rel_grad.at[peer], rel_got.at[s], a_send, a_recv)
    rel_got[s] = rel_grad[s]
    grad_dest = jnp.concatenate(
        [rel_re * grad_re + rel_im * grad_im, rel_re * grad_im - rel_im * grad_re], axis=0
    )
    dest_high, dest_low = halves(grad_dest)
    visit_grad = lax.dot_general(dest_high, hot_dest, NT, preferred_element_type=f32) + lax.dot_general(
        dest_low, hot_dest, NT, preferred_element_type=f32
    )
    share = jnp.dot(hot_neg[...], weight, preferred_element_type=f32) + pos_weight * hot_source.astype(f32)
    share_high, share_low = halves(share)
    home_grad = lax.dot_general(trans, share_high, NT, preferred_element_type=f32) + lax.dot_general(
        trans, share_low, NT, preferred_element_type=f32
    )
    for c in range(4):
        grads[c, 0] = home_grad[:, c * 256 : (c + 1) * 256]
        grads[c, 1] = visit_grad[:, c * 256 : (c + 1) * 256]

    for copy in swaps:
        copy.wait_recv()
    for c in range(4):
        high, rest = halves(rel_got[c])
        both[:QROWS, c * SHARE : (c + 1) * SHARE] = high
        both[QROWS:, c * SHARE : (c + 1) * SHARE] = rest

    def scatter(chunk, zz):
        hot_lanes(low_hot, hot, group, chunk * 32 + lax.rem(zz + 8, 8) * 4)
        sums = lax.dot_general(both[...], hot[...], NT, preferred_element_type=f32)
        sums = sums[:QROWS] + sums[QROWS:]
        return [sums[:, k * 128 : (k + 1) * 128] for k in range(4)]

    back = {}

    def ring(dist):
        for chunk in (0, 1):
            for way in ("r", "l"):
                if dist > FAR[(way, chunk)]:
                    continue
                buf, got, send, recv = (
                    (r_buf, r_got, rr_send, rr_recv) if way == "r" else (l_buf, l_got, ll_send, ll_recv)
                )
                value = scatter(chunk, z + dist if way == "r" else z - dist)
                if dist < FAR[(way, chunk)]:
                    back[(way, chunk, dist + 1)].wait_recv()
                    value = [v + got[chunk, dist, k].astype(f32) for k, v in enumerate(value)]
                for k in range(4):
                    buf[chunk, dist - 1, k] = value[k].astype(bf16)
                back[(way, chunk, dist)] = go(
                    remote(
                        buf.at[chunk, dist - 1], got.at[chunk, dist - 1],
                        send.at[chunk, dist - 1], recv.at[chunk, dist - 1],
                        right if way == "r" else left,
                    )
                )

    m_copies = {}
    o_copies = {}

    def to_mate(k):
        for i, row in ((1, across_mate), (0, mate_span)):
            m_copies[(i, k)] = go(remote(grads.at[row, k], m_got.at[i, k], m_send.at[i, k], m_recv.at[i, k], mate))

    def cross(k):
        m_copies[(1, k)].wait_recv()
        o_buf[k] = (grads[across_span, k] + m_got[1, k]).astype(bf16)
        o_copies[k] = go(remote(o_buf.at[k], o_got.at[k], o_send.at[k], o_recv.at[k], across))

    def summed(k):
        m_copies[(0, k)].wait_recv()
        o_copies[k].wait_recv()
        return grads[s, k] + m_got[0, k] + o_got[k].astype(f32)

    ring(4)
    to_mate(1)
    ring(3)
    to_mate(0)
    cross(1)
    ring(2)
    cross(0)
    visit_sum[...] = summed(1).astype(bf16)
    moves.append(go(remote(visit_sum, visit_grad_ref, v_send.at[2], v_recv.at[2], after)))
    ring(1)
    x_copies = []
    for chunk in (0, 1):
        near = scatter(chunk, z)
        back[("r", chunk, 1)].wait_recv()
        back[("l", chunk, 1)].wait_recv()
        for k in range(4):
            row_sum[chunk, k] = near[k] + r_got[chunk, 0, k].astype(f32) + l_got[chunk, 0, k].astype(f32)
        for d in (1, 2, 3):
            x_copies.append(
                go(
                    remote(
                        row_sum.at[chunk, lax.rem(x + d, 4)], x_got.at[chunk, d - 1],
                        xx_send.at[chunk, d - 1], xx_recv.at[chunk, d - 1], x_peers[d - 1],
                    )
                )
            )
    home_grad_ref[...] = summed(0)
    for copy in x_copies:
        copy.wait_recv()
    for chunk in (0, 1):
        x_sum[chunk] = row_sum[chunk, x] + x_got[chunk, 0] + x_got[chunk, 1] + x_got[chunk, 2]
    y_copy = go(remote(x_sum.at[yo], y_got, yy_send, yy_recv, y_peer))
    y_copy.wait_recv()
    quarter_ref[s] = x_sum[yh] + y_got[...]
    for copy in to_span(lambda peer: quarter_ref.at[s], quarter_ref.at[s], q_send, q_recv) + moves:
        copy.wait_recv()
    for copy in started:
        copy.wait_send()


def bucket_round(src, rel, dst, count, neg_rows, home, visit, visit_state, relation):
    dma = pltpu.SemaphoreType.DMA
    bf16, f32, i32 = jnp.bfloat16, jnp.float32, jnp.int32
    pair = (2,) + home.shape
    quarters = (4, QROWS, SHARE)
    ring = pltpu.VMEM((2, 4, 4, QROWS, 128), bf16)
    rows = home.shape[0]
    return pl.pallas_call(
        round_kernel,
        out_shape=(
            jax.ShapeDtypeStruct(home.shape, f32),
            jax.ShapeDtypeStruct(visit.shape, f32),
            jax.ShapeDtypeStruct(visit_state.shape, f32),
            jax.ShapeDtypeStruct(visit.shape, bf16),
            jax.ShapeDtypeStruct((4, QROWS, 128), f32),
        ),
        in_specs=[VMEM] * 9,
        out_specs=(VMEM,) * 5,
        scratch_shapes=[
            pltpu.VMEM(pair, bf16), pltpu.VMEM((4,) + pair, bf16),
            pltpu.VMEM((4, QROWS, 128), bf16), pltpu.VMEM((3, QROWS, 128), bf16),
            pltpu.VMEM((4, 8, 1024), i32), pltpu.VMEM((2, 8, 4, QROWS, 128), bf16),
            pltpu.VMEM((128, LIVE), bf16), pltpu.VMEM((512, LIVE), bf16), pltpu.VMEM((QROWS, LIVE), f32),
            pltpu.VMEM(quarters, bf16), pltpu.VMEM(quarters, bf16),
            pltpu.VMEM((1024, 1024), bf16), pltpu.VMEM((rows, 1024), bf16),
            pltpu.VMEM(quarters, f32), pltpu.VMEM(quarters, f32), pltpu.VMEM((2 * QROWS, LIVE), bf16),
            pltpu.VMEM((4,) + pair, f32),
            ring, ring, ring, ring,
            pltpu.VMEM((2, 4, QROWS, 128), f32), pltpu.VMEM((2, 3, QROWS, 128), f32),
            pltpu.VMEM((2, QROWS, 128), f32), pltpu.VMEM((QROWS, 128), f32),
            pltpu.VMEM((2,) + pair, f32), pltpu.VMEM(pair, bf16), pltpu.VMEM(pair, bf16),
            pltpu.VMEM(visit.shape, bf16),
            dma((3,)), dma((3,)), dma((3,)), dma((3,)), dma((2, 3)), dma((2, 3)), dma, dma,
            dma((2, 3)), dma((2, 3)), dma((2, 4)), dma((2, 4)), dma((2, 4)), dma((2, 4)),
            dma((3,)), dma((3,)), dma((3,)), dma((3,)), dma((3,)), dma((3,)),
            dma((2, 4)), dma((2, 4)), dma((2, 4)), dma((2, 4)), dma((2, 3)), dma((2, 3)),
            dma, dma, dma((3,)), dma((3,)), dma((2, 2)), dma((2, 2)), dma((2,)), dma((2,)),
        ],
        compiler_params=params(0),
        name="bucket_round",
    )(src, rel, dst, count, neg_rows, home, visit, visit_state, relation)


def adagrad(table, state, grad_in, axis):
    state_new = state + jnp.sum(grad_in * grad_in, axis=axis, keepdims=True) * (1.0 / grad_in.shape[axis])
    return table - LEARN_RATE * grad_in / (jnp.sqrt(state_new) + ADAGRAD_EPS), state_new


def update_kernel(
    home_grad_ref, home_ref, home_state_ref, visit_grad_ref, visit_ref, visit_state_ref,
    quarter_ref, relation_ref, relation_state_ref,
    home_out, home_state_out, visit_out, visit_state_out, relation_out, relation_state_out,
):
    f32 = jnp.float32
    s = lax.axis_index("span")
    home_out[...], home_state_out[...] = adagrad(home_ref[...], home_state_ref[...], home_grad_ref[...], 0)
    visit_out[...], visit_state_out[...] = adagrad(
        visit_ref[...], visit_state_ref[...], visit_grad_ref[...].astype(f32), 0
    )
    res, ims = [], []
    for c in range(4):
        part = quarter_ref[c]
        own = jnp.zeros((QROWS, 32), f32)
        for k in range(4):
            own = jnp.where(s == k, part[:, 32 * k : 32 * (k + 1)], own)
        res.append(own[:QPART])
        ims.append(own[QIM : QIM + QPART])
    grad = jnp.concatenate(res + ims, axis=0)
    state = relation_state_ref[...] + jnp.sum(grad * grad, axis=0, keepdims=True)[:, :OWN_RELS] * (1.0 / grad.shape[0])
    step = grad[:, :OWN_RELS] / (jnp.sqrt(state) + ADAGRAD_EPS)
    step = jnp.concatenate([step, jnp.zeros((grad.shape[0], 32 - OWN_RELS), f32)], axis=1).T[:OWN_RELS]
    relation_out[...] = relation_ref[...] - LEARN_RATE * step
    relation_state_out[...] = state


def update(*arrays):
    shape = lambda a: jax.ShapeDtypeStruct(a.shape, jnp.float32)
    return pl.pallas_call(
        update_kernel,
        out_shape=tuple(shape(arrays[i]) for i in (1, 2, 4, 5, 7, 8)),
        in_specs=[VMEM] * 9,
        out_specs=(VMEM,) * 6,
        compiler_params=params(),
        name="update",
    )(*arrays)


def shards(
    home_table, home_state, visit_table, visit_state, relation_table, relation_state,
    edge_src, edge_rel, edge_dst, edge_count, neg_rows,
):
    home_grad, moved, moved_state, moved_grad, quarters = bucket_round(
        edge_src[0], edge_rel[0], edge_dst[0], edge_count, neg_rows,
        home_table, visit_table, visit_state[None], relation_table.T,
    )
    new_home, new_home_state, new_visit, new_visit_state, new_relation, new_relation_state = update(
        home_grad, home_table, home_state[None], moved_grad, moved, moved_state,
        quarters, relation_table.T, relation_state[None],
    )
    return (new_home, new_home_state[0], new_visit, new_visit_state[0], new_relation.T, new_relation_state[0])


def solution(mesh):
    cols = P(None, ("blk", "span"))
    rows = P(("blk", "span"))
    slot = P("blk", "span", None)
    return jax.shard_map(
        shards,
        mesh=mesh,
        in_specs=(cols, rows, cols, rows, cols, rows, slot, slot, slot, P("blk", "span"), P("blk", None)),
        out_specs=(cols, rows, cols, rows, cols, rows),
        check_vma=False,
    )
```

time: 117 us -> 101 us (0.86)
  local copies, waits for them, and re-layouts: 9.9 us -> 0 us
  Pallas kernels: 103 us -> 98 us
  other arithmetic: 1.32 us -> 0 us
    unnamed x8 -> x0, local copies, waits for them, and re-layouts: 8.64 us -> none
    pallas_call x2, Pallas kernels: 103 us -> 98 us  [the longest x1 95 us: bucket_round(): pl.pallas_call(round_kernel, out_shape=(jax.ShapeDtypeStruct(home.shape,...]
    add x1 -> x0, other arithmetic: 1.32 us -> none  [shards(): spot = edge_rel[0] // OWN_RELS * 32 + edge_rel[0] % OWN_RELS]
    slice x1 -> x0, local copies, waits for them, and re-layouts: 1.26 us -> none  [shards(): moved_state[0]]
where the time goes in v3:
time: 101 us; the launch traced here: 99.3 us
  Pallas kernels  98 us (97%)
  between operations  1.29 us (1%)
    pallas_call x1, Pallas kernels, bucket_round(): pl.pallas_call(round_kernel, out_shape=(jax.ShapeDtypeStruct(home.shape,...  95 us
    pallas_call x1, Pallas kernels, update(): pl.pallas_call(update_kernel, out_shape=tuple((shape(arrays[i]) for i in...  3.05 us

profile of v3, /device:TPU:1, one launch (start us, length us, event | category | flops | bytes accessed | tf_op | source)
XLA Modules:
  0.0 99.3 jit_solution(11097009883810136745)
XLA Ops:
  1.3 95.0 %bucket_round.1 = (f32[400,256]{1,0:T(8,128)}, f32[400,256]{1,0:T(8,128)}, f32[1,256]{1,0:T(1,128)}, bf16[400,256]{1,0:T(8,128)(2,1)}, f32[4,112,128]{2,1,0:T(8,128)}) custom-call(s32[1,1024]{1,0:T(1,128)} %bitcast.13, s32[1,1024]{1,0:T(1,128)} %bitcast.14, s32[1,1024]{1,0:T(1,128)} %bitcast.15, s32[1,1]{1,0:T(1,128)S(6)} %copy.17.count_ref, ...), custom_call_target="tpu_custom_call" | custom-call | tf_op jit(solution)/shard_map/bucket_round/pallas_call | solution.py:394
  96.2 3.1 %update.1 = (f32[400,256]{1,0:T(8,128)}, f32[1,256]{1,0:T(1,128)}, f32[400,256]{1,0:T(8,128)}, f32[1,256]{1,0:T(1,128)}, f32[29,400]{1,0:T(8,128)}, /*index=5*/f32[1,29]{1,0:T(1,128)}) custom-call(f32[400,256]{1,0:T(8,128)} %get-tuple-element.17.home_grad_ref, f32[400,256]{1,0:T(8,128)} %home_ref.3, f32[1,256]{1,0:T(1,128)} %bitcast.16, ...), custom_call_target="tpu_custom_call" | custom-call | tf_op jit(solution)/shard_map/update/pallas_call | solution.py:464

commit v4 on v3

--- a/solution.py
+++ b/solution.py
@@ -82,11 +82,13 @@
     home_grad_ref, visit_out, visit_state_out, visit_grad_ref, quarter_ref,
     low, low_all, piece, got_piece, index, table, low_hot, hot, total, mine, picked,
     hot_neg, negatives, rel_grad, rel_got, both, grads,
-    r_buf, r_got, l_buf, l_got, row_sum, x_got, x_sum, y_got, m_got, o_buf, o_got, visit_sum,
+    r_buf, r_got, l_buf, l_got, row_sum, x_got, x_sum, y_got, q_buf, m_got, o_buf, o_got, visit_sum,
+    negatives_t, kept, cast, x_in, one_buf, one_got,
     i_send, i_recv, p_send, p_recv, h_send, h_recv, y_send, y_recv, x_send, x_recv,
     r_send, r_recv, l_send, l_recv, k_send, k_recv, v_send, v_recv, a_send, a_recv,
     rr_send, rr_recv, ll_send, ll_recv, xx_send, xx_recv, yy_send, yy_recv, q_send, q_recv,
-    m_send, m_recv, o_send, o_recv,
+    m_send, m_recv, o_send, o_recv, b_send, b_recv, c_send, c_recv, w_send, w_recv,
+    xb_send, xb_recv, e_send, e_recv,
 ):
     f32, bf16 = jnp.float32, jnp.bfloat16
     yh, z, x, s = place()
@@ -107,19 +109,15 @@
     peers = span_peers + x_peers + [y_peer, right, left, after, before]
     greet(peers)
 
-    operators = jnp.concatenate([relation_ref[...], jnp.zeros((32 - OWN_RELS, 8 * QPART), f32)], axis=0).T
-    middle = operators.shape[0] // 2
-    pad = jnp.zeros((QIM - QPART, 32), f32)
+    middle = 4 * QPART
+    spare = jnp.zeros((32 - OWN_RELS, 2 * middle), f32)
+    operators = jnp.concatenate([relation_ref[...], spare], axis=0)
     for c in range(4):
-        re = operators[c * QPART : (c + 1) * QPART]
-        im = operators[middle + c * QPART : middle + (c + 1) * QPART]
-        quarter = jnp.concatenate([re, pad, im, pad], axis=0)
-        placed = jnp.zeros((QROWS, 128), f32)
-        for k in range(4):
-            parts = [jnp.zeros((QROWS, 32), f32)] * 4
-            parts[k] = quarter
-            placed = jnp.where(s == k, jnp.concatenate(parts, axis=1), placed)
-        piece[c] = placed.astype(bf16)
+        re = operators[:, c * QPART : (c + 1) * QPART]
+        im = operators[:, middle + c * QPART : middle + (c + 1) * QPART]
+        pad = jnp.zeros((32, QIM - QPART), f32)
+        rest = jnp.zeros((32, 128 - QIM - QPART), f32)
+        piece[c] = jnp.concatenate([re, pad, im, rest], axis=1).astype(bf16)
     rel = rel_ref[...]
     owner = jnp.right_shift(rel * 4520, 17)
     index[s] = jnp.concatenate(
@@ -149,26 +147,34 @@
             for d in (1, 2, 3)
         ]
 
-    pieces = [
-        go(remote(piece.at[lax.rem(s + d, 4)], got_piece.at[d - 1], p_send.at[d - 1], p_recv.at[d - 1], span_peers[d - 1]))
-        for d in (1, 2, 3)
-    ]
+    pieces = to_span(lambda peer: piece.at[peer], got_piece.at[s], p_send, p_recv)
     lists = to_span(lambda peer: index.at[s], index.at[s], i_send, i_recv)
+    got_piece[s] = piece[s]
     for copy in pieces:
         copy.wait_recv()
-    table[yh, z, x] = piece[s] + got_piece[0] + got_piece[1] + got_piece[2]
+    block = jnp.concatenate([got_piece[c].astype(f32) for c in range(4)], axis=0).T
+    table[yh, z, x] = block[:QROWS].astype(bf16)
 
     own = table.at[yh, z, x]
     other = table.at[yo, z, x]
     y_copy = go(remote(own, own, y_send, y_recv, y_peer))
-    x_copies = [[], []]
-    for d in (1, 2, 3):
-        x_copies[0].append(go(remote(own, own, x_send.at[0, d - 1], x_recv.at[0, d - 1], x_peers[d - 1])))
+    x_copies = [
+        go(remote(own, own, x_send.at[d - 1], x_recv.at[d - 1], x_peers[d - 1])) for d in (1, 2, 3)
+    ]
+    lows = [[], []]
+    for k in (0, 1):
+        for number, peer in enumerate((across, mate)):
+            lows[k].append(
+                go(remote(low.at[k], low_all.at[s, k], h_send.at[k, number], h_recv.at[k, number], peer))
+            )
+
+    def relay(k):
+        lows[k][0].wait_recv()
+        ref = low_all.at[across_span, k]
+        lows[k].append(go(remote(ref, ref, h_send.at[k, 2], h_recv.at[k, 2], mate)))
+
     for copy in lists:
         copy.wait_recv()
-    y_copy.wait_recv()
-    for d in (1, 2, 3):
-        x_copies[1].append(go(remote(other, other, x_send.at[1, d - 1], x_recv.at[1, d - 1], x_peers[d - 1])))
 
     at = lax.broadcasted_iota(jnp.int32, (8, LIVE), 1)
     kind = lax.broadcasted_iota(jnp.int32, (8, LIVE), 0)
@@ -203,36 +209,63 @@
         total[...] += jnp.dot(block, hot[...], preferred_element_type=f32)
 
     flying = {}
-    lows = [[], []]
+    turns = {"r": 4, "l": 3}
+    rows = {}
+
+    def pass_on(way, step, key, send, recv, ref):
+        flying[(key, way, step)] = go(remote(ref, ref, send, recv, right if way == "r" else left))
+
+    def along_x(number, ref):
+        rows[number] = [
+            go(remote(ref, ref, w_send.at[number, d - 1], w_recv.at[number, d - 1], x_peers[d - 1]))
+            for d in (1, 2, 3)
+        ]
+
+    def gather_row(number, zz):
+        for copy in rows[number]:
+            copy.wait_recv()
+        gather(1, zz)
+
     for step in range(5):
-        for chunk in (0, 1):
-            if step == 0:
-                for copy in x_copies[chunk]:
-                    copy.wait_recv()
+        if step == 0:
+            y_copy.wait_recv()
+            along_x(0, other)
+        for way in ("r", "l"):
+            zz = z - step if way == "r" else z + step
+            ref = table.at[yo, lax.rem(zz + 8, 8), x]
+            if 1 <= step <= turns[way]:
+                flying[("other", way, step - 1)].wait_recv()
+            if step < turns[way]:
+                send, recv = (b_send, b_recv) if way == "r" else (c_send, c_recv)
+                pass_on(way, step, "other", send.at[step], recv.at[step], ref)
+            if 1 <= step <= turns[way]:
+                along_x(step if way == "r" else 4 + step, ref)
+        if step == 0:
+            for copy in x_copies:
+                copy.wait_recv()
+        for part in (0, 1):
             for way in ("r", "l"):
-                if 1 <= step <= FAR[(way, chunk)]:
-                    flying[(way, chunk, step - 1)].wait_recv()
-                if step < FAR[(way, chunk)]:
+                if 1 <= step <= FAR[(way, part)]:
+                    flying[(part, way, step - 1)].wait_recv()
+                if step < FAR[(way, part)]:
                     zz = z - step if way == "r" else z + step
+                    ref = table.at[yh, lax.rem(zz + 8, 8), pl.ds(2 * part, 2)]
                     send, recv = (r_send, r_recv) if way == "r" else (l_send, l_recv)
-                    ref = table.at[half(chunk), lax.rem(zz + 8, 8)]
-                    flying[(way, chunk, step)] = go(
-                        remote(ref, ref, send.at[chunk, step], recv.at[chunk, step], right if way == "r" else left)
-                    )
-            if step == 0:
-                lows[chunk] = to_span(lambda peer: low.at[chunk], low_all.at[s, chunk], h_send.at[chunk], h_recv.at[chunk])
-                gather(chunk, z)
+                    pass_on(way, step, part, send.at[part, step], recv.at[part, step], ref)
+        if step == 0:
+            gather(0, z)
+        else:
+            gather(0, z - step)
+            if step < 4:
+                gather(0, z + step)
+            if step == 1:
+                gather_row(0, z)
             else:
-                for way in ("r", "l"):
-                    if step <= FAR[(way, chunk)]:
-                        gather(chunk, z - step if way == "r" else z + step)
-            if step == 3 and chunk == 0:
-                for copy in lows[0]:
-                    copy.wait_recv()
-                hot_neg[...] = one_hot(1024, neg_ref[...])
-            if step == 3 and chunk == 1:
-                home = jnp.concatenate([low_all[c, 0] for c in range(4)], axis=1)
-                negatives[...] = jnp.dot(home, hot_neg[...], preferred_element_type=f32).astype(bf16)
+                gather_row(step - 1, z - step + 1)
+                gather_row(step + 3, z + step - 1)
+        if step in (1, 2):
+            relay(step - 1)
+    gather_row(4, z - 4)
     for c in range(4):
         mine[c] = total[:, c * SHARE : (c + 1) * SHARE].astype(bf16)
     picks = to_span(lambda peer: mine.at[peer], picked.at[s], k_send, k_recv)
@@ -242,7 +275,14 @@
         go(remote(visit_state_ref, visit_state_out, v_send.at[1], v_recv.at[1], after)),
     ]
 
-    for copy in lows[1]:
+    for copy in lows[0][1:]:
+        copy.wait_recv()
+    hot_neg[...] = one_hot(1024, neg_ref[...])
+    home = jnp.concatenate([low_all[c, 0] for c in range(4)], axis=1)
+    found = jnp.dot(home, hot_neg[...], preferred_element_type=f32)
+    negatives[...] = found.astype(bf16)
+    negatives_t[...] = found.T.astype(bf16)
+    for copy in lows[1][1:]:
         copy.wait_recv()
     visit = jnp.concatenate([low_all[c, 1] for c in range(4)], axis=1)
     live = share_slots[3:4, :].astype(f32)
@@ -260,7 +300,7 @@
         [rel_re * dest_re - rel_im * dest_im, rel_re * dest_im + rel_im * dest_re], axis=0
     ).astype(bf16)
     positive = jnp.sum(source * trans.astype(f32), axis=0, keepdims=True)
-    score = lax.dot_general(negatives[...], trans, (((0,), (0,)), ((), ())), preferred_element_type=f32)
+    score = jnp.dot(negatives_t[...], trans, preferred_element_type=f32)
     pos_weight = -live * jax.nn.sigmoid(-positive)
     weight = (live * jax.nn.sigmoid(score) * (1.0 / 1024.0)).astype(bf16)
     pull = jnp.dot(negatives[...], weight, preferred_element_type=f32)
@@ -270,10 +310,15 @@
     out_im = dest_re * grad_im - dest_im * grad_re
     pad = jnp.zeros((QIM - QPART, SHARE), f32)
     for c in range(4):
-        rows = slice(c * QPART, (c + 1) * QPART)
-        rel_grad[c] = jnp.concatenate([out_re[rows], pad, out_im[rows], pad], axis=0)
-    swaps = to_span(lambda peer: rel_grad.at[peer], rel_got.at[s], a_send, a_recv)
-    rel_got[s] = rel_grad[s]
+        part = slice(c * QPART, (c + 1) * QPART)
+        high, rest = halves(jnp.concatenate([out_re[part], pad, out_im[part], pad], axis=0))
+        rel_grad[0, c] = high
+        rel_grad[1, c] = rest
+    swaps = [
+        to_span(lambda peer: rel_grad.at[i, peer], rel_got.at[i, s], a_send.at[i], a_recv.at[i]) for i in (0, 1)
+    ]
+    for i in (0, 1):
+        rel_got[i, s] = rel_grad[i, s]
     grad_dest = jnp.concatenate(
         [rel_re * grad_re + rel_im * grad_im, rel_re * grad_im - rel_im * grad_re], axis=0
     )
@@ -290,42 +335,87 @@
         grads[c, 0] = home_grad[:, c * 256 : (c + 1) * 256]
         grads[c, 1] = visit_grad[:, c * 256 : (c + 1) * 256]
 
-    for copy in swaps:
-        copy.wait_recv()
-    for c in range(4):
-        high, rest = halves(rel_got[c])
-        both[:QROWS, c * SHARE : (c + 1) * SHARE] = high
-        both[QROWS:, c * SHARE : (c + 1) * SHARE] = rest
-
-    def scatter(chunk, zz):
-        hot_lanes(low_hot, hot, group, chunk * 32 + lax.rem(zz + 8, 8) * 4)
-        sums = lax.dot_general(both[...], hot[...], NT, preferred_element_type=f32)
-        sums = sums[:QROWS] + sums[QROWS:]
+    def take(i):
+        for copy in swaps[i]:
+            copy.wait_recv()
+        for c in range(4):
+            both[i * QROWS : (i + 1) * QROWS, c * SHARE : (c + 1) * SHARE] = rel_got[i, c]
+
+    def scatter(chunk, zz, fine=True):
+        hot_lanes(low_hot, hot, group, half(chunk) * 32 + lax.rem(zz + 8, 8) * 4)
+        if fine:
+            sums = lax.dot_general(both[...], hot[...], NT, preferred_element_type=f32)
+            sums = sums[:QROWS] + sums[QROWS:]
+        else:
+            sums = lax.dot_general(both[:QROWS], hot[...], NT, preferred_element_type=f32)
         return [sums[:, k * 128 : (k + 1) * 128] for k in range(4)]
 
     back = {}
 
     def ring(dist):
-        for chunk in (0, 1):
-            for way in ("r", "l"):
-                if dist > FAR[(way, chunk)]:
+        value = None
+        for way in ("r", "l"):
+            zz = z + dist if way == "r" else z - dist
+            buf, got, send, recv = (
+                (r_buf, r_got, rr_send, rr_recv) if way == "r" else (l_buf, l_got, ll_send, ll_recv)
+            )
+            if dist < 4 or value is None:
+                value = scatter(0, zz, dist < 4)
+            for part in (0, 1):
+                if dist > FAR[(way, part)]:
                     continue
-                buf, got, send, recv = (
-                    (r_buf, r_got, rr_send, rr_recv) if way == "r" else (l_buf, l_got, ll_send, ll_recv)
-                )
-                value = scatter(chunk, z + dist if way == "r" else z - dist)
-                if dist < FAR[(way, chunk)]:
-                    back[(way, chunk, dist + 1)].wait_recv()
-                    value = [v + got[chunk, dist, k].astype(f32) for k, v in enumerate(value)]
-                for k in range(4):
-                    buf[chunk, dist - 1, k] = value[k].astype(bf16)
-                back[(way, chunk, dist)] = go(
+                if dist < FAR[(way, part)]:
+                    back[(part, way, dist + 1)].wait_recv()
+                for k in (0, 1):
+                    here = value[2 * part + k]
+                    if dist < FAR[(way, part)]:
+                        here = here + got[part, dist, k].astype(f32)
+                    buf[part, dist - 1, k] = here.astype(bf16)
+                back[(part, way, dist)] = go(
                     remote(
-                        buf.at[chunk, dist - 1], got.at[chunk, dist - 1],
-                        send.at[chunk, dist - 1], recv.at[chunk, dist - 1],
+                        buf.at[part, dist - 1], got.at[part, dist - 1],
+                        send.at[part, dist - 1], recv.at[part, dist - 1],
                         right if way == "r" else left,
                     )
                 )
+
+    x_rows = {}
+
+    def sow(number, zz, fine=True):
+        value = scatter(1, zz, fine)
+        for k in range(4):
+            kept[number, k] = value[k]
+            cast[number, k] = value[k].astype(bf16)
+        x_rows[number] = [
+            go(
+                remote(
+                    cast.at[number, lax.rem(x + d, 4)], x_in.at[number, d - 1],
+                    xb_send.at[number, d - 1], xb_recv.at[number, d - 1], x_peers[d - 1],
+                )
+            )
+            for d in (1, 2, 3)
+        ]
+
+    def reap(number):
+        for copy in x_rows[number]:
+            copy.wait_recv()
+        return kept[number, x] + sum(x_in[number, d].astype(f32) for d in range(3))
+
+    def ring_row(dist):
+        for i, way in enumerate(("r", "l")):
+            if dist > turns[way]:
+                continue
+            value = reap(dist if way == "r" else 4 + dist)
+            if dist < turns[way]:
+                back[("other", way, dist + 1)].wait_recv()
+                value = value + one_got[i, dist]
+            one_buf[i, dist - 1] = value
+            back[("other", way, dist)] = go(
+                remote(
+                    one_buf.at[i, dist - 1], one_got.at[i, dist - 1],
+                    e_send.at[i, dist - 1], e_recv.at[i, dist - 1], right if way == "r" else left,
+                )
+            )
 
     m_copies = {}
     o_copies = {}
@@ -344,41 +434,61 @@
         o_copies[k].wait_recv()
         return grads[s, k] + m_got[0, k] + o_got[k].astype(f32)
 
+    take(0)
+    sow(4, z + 4, False)
     ring(4)
     to_mate(1)
+    take(1)
+    sow(3, z + 3)
+    sow(7, z - 3)
     ring(3)
+    ring_row(4)
     to_mate(0)
+    sow(2, z + 2)
+    sow(6, z - 2)
+    ring(2)
+    ring_row(3)
     cross(1)
-    ring(2)
+    sow(1, z + 1)
+    sow(5, z - 1)
+    ring(1)
+    ring_row(2)
     cross(0)
     visit_sum[...] = summed(1).astype(bf16)
     moves.append(go(remote(visit_sum, visit_grad_ref, v_send.at[2], v_recv.at[2], after)))
-    ring(1)
-    x_copies = []
-    for chunk in (0, 1):
-        near = scatter(chunk, z)
-        back[("r", chunk, 1)].wait_recv()
-        back[("l", chunk, 1)].wait_recv()
-        for k in range(4):
-            row_sum[chunk, k] = near[k] + r_got[chunk, 0, k].astype(f32) + l_got[chunk, 0, k].astype(f32)
-        for d in (1, 2, 3):
-            x_copies.append(
-                go(
-                    remote(
-                        row_sum.at[chunk, lax.rem(x + d, 4)], x_got.at[chunk, d - 1],
-                        xx_send.at[chunk, d - 1], xx_recv.at[chunk, d - 1], x_peers[d - 1],
-                    )
-                )
+    sow(0, z)
+    ring_row(1)
+    near = scatter(0, z)
+    for part in (0, 1):
+        back[(part, "r", 1)].wait_recv()
+        back[(part, "l", 1)].wait_recv()
+        for k in (0, 1):
+            row_sum[2 * part + k] = (
+                near[2 * part + k] + r_got[part, 0, k].astype(f32) + l_got[part, 0, k].astype(f32)
             )
+    x_copies = [
+        go(
+            remote(
+                row_sum.at[lax.rem(x + d, 4)], x_got.at[d - 1],
+                xx_send.at[d - 1], xx_recv.at[d - 1], x_peers[d - 1],
+            )
+        )
+        for d in (1, 2, 3)
+    ]
+    for way in ("r", "l"):
+        back[("other", way, 1)].wait_recv()
+    x_sum[...] = reap(0) + one_got[0, 0] + one_got[1, 0]
+    y_copy = go(remote(x_sum, y_got, yy_send, yy_recv, y_peer))
     home_grad_ref[...] = summed(0)
     for copy in x_copies:
         copy.wait_recv()
-    for chunk in (0, 1):
-        x_sum[chunk] = row_sum[chunk, x] + x_got[chunk, 0] + x_got[chunk, 1] + x_got[chunk, 2]
-    y_copy = go(remote(x_sum.at[yo], y_got, yy_send, yy_recv, y_peer))
+    here = row_sum[x] + x_got[0] + x_got[1] + x_got[2]
     y_copy.wait_recv()
-    quarter_ref[s] = x_sum[yh] + y_got[...]
-    for copy in to_span(lambda peer: quarter_ref.at[s], quarter_ref.at[s], q_send, q_recv) + moves:
+    turned = jnp.concatenate([here + y_got[...], jnp.zeros((128 - QROWS, 128), f32)], axis=0).T
+    for c in range(4):
+        q_buf[c] = turned[32 * c : 32 * (c + 1)]
+    quarter_ref[s] = q_buf[s]
+    for copy in to_span(lambda peer: q_buf.at[peer], quarter_ref.at[s], q_send, q_recv) + moves:
         copy.wait_recv()
     for copy in started:
         copy.wait_send()
@@ -389,7 +499,8 @@
     bf16, f32, i32 = jnp.bfloat16, jnp.float32, jnp.int32
     pair = (2,) + home.shape
     quarters = (4, QROWS, SHARE)
-    ring = pltpu.VMEM((2, 4, 4, QROWS, 128), bf16)
+    ring = pltpu.VMEM((2, 4, 2, QROWS, 128), bf16)
+    lone = pltpu.VMEM((2, 4, QROWS, 128), f32)
     rows = home.shape[0]
     return pl.pallas_call(
         round_kernel,
@@ -398,29 +509,33 @@
             jax.ShapeDtypeStruct(visit.shape, f32),
             jax.ShapeDtypeStruct(visit_state.shape, f32),
             jax.ShapeDtypeStruct(visit.shape, bf16),
-            jax.ShapeDtypeStruct((4, QROWS, 128), f32),
+            jax.ShapeDtypeStruct((4, 32, 128), f32),
         ),
         in_specs=[VMEM] * 9,
         out_specs=(VMEM,) * 5,
         scratch_shapes=[
             pltpu.VMEM(pair, bf16), pltpu.VMEM((4,) + pair, bf16),
-            pltpu.VMEM((4, QROWS, 128), bf16), pltpu.VMEM((3, QROWS, 128), bf16),
+            pltpu.VMEM((4, 32, 128), bf16), pltpu.VMEM((4, 32, 128), bf16),
             pltpu.VMEM((4, 8, 1024), i32), pltpu.VMEM((2, 8, 4, QROWS, 128), bf16),
             pltpu.VMEM((128, LIVE), bf16), pltpu.VMEM((512, LIVE), bf16), pltpu.VMEM((QROWS, LIVE), f32),
             pltpu.VMEM(quarters, bf16), pltpu.VMEM(quarters, bf16),
             pltpu.VMEM((1024, 1024), bf16), pltpu.VMEM((rows, 1024), bf16),
-            pltpu.VMEM(quarters, f32), pltpu.VMEM(quarters, f32), pltpu.VMEM((2 * QROWS, LIVE), bf16),
+            pltpu.VMEM((2,) + quarters, bf16), pltpu.VMEM((2,) + quarters, bf16), pltpu.VMEM((2 * QROWS, LIVE), bf16),
             pltpu.VMEM((4,) + pair, f32),
             ring, ring, ring, ring,
-            pltpu.VMEM((2, 4, QROWS, 128), f32), pltpu.VMEM((2, 3, QROWS, 128), f32),
-            pltpu.VMEM((2, QROWS, 128), f32), pltpu.VMEM((QROWS, 128), f32),
+            pltpu.VMEM((4, QROWS, 128), f32), pltpu.VMEM((3, QROWS, 128), f32),
+            pltpu.VMEM((QROWS, 128), f32), pltpu.VMEM((QROWS, 128), f32), pltpu.VMEM((4, 32, 128), f32),
             pltpu.VMEM((2,) + pair, f32), pltpu.VMEM(pair, bf16), pltpu.VMEM(pair, bf16),
             pltpu.VMEM(visit.shape, bf16),
+            pltpu.VMEM((1024, rows), bf16), pltpu.VMEM((8, 4, QROWS, 128), f32), pltpu.VMEM((8, 4, QROWS, 128), bf16),
+            pltpu.VMEM((8, 3, QROWS, 128), bf16), lone, lone,
             dma((3,)), dma((3,)), dma((3,)), dma((3,)), dma((2, 3)), dma((2, 3)), dma, dma,
-            dma((2, 3)), dma((2, 3)), dma((2, 4)), dma((2, 4)), dma((2, 4)), dma((2, 4)),
-            dma((3,)), dma((3,)), dma((3,)), dma((3,)), dma((3,)), dma((3,)),
-            dma((2, 4)), dma((2, 4)), dma((2, 4)), dma((2, 4)), dma((2, 3)), dma((2, 3)),
+            dma((3,)), dma((3,)), dma((2, 4)), dma((2, 4)), dma((2, 4)), dma((2, 4)),
+            dma((3,)), dma((3,)), dma((3,)), dma((3,)), dma((2, 3)), dma((2, 3)),
+            dma((2, 4)), dma((2, 4)), dma((2, 4)), dma((2, 4)), dma((3,)), dma((3,)),
             dma, dma, dma((3,)), dma((3,)), dma((2, 2)), dma((2, 2)), dma((2,)), dma((2,)),
+            dma((4,)), dma((4,)), dma((4,)), dma((4,)), dma((8, 3)), dma((8, 3)),
+            dma((8, 3)), dma((8, 3)), dma((2, 4)), dma((2, 4)),
         ],
         compiler_params=params(0),
         name="bucket_round",
@@ -438,25 +553,19 @@
     home_out, home_state_out, visit_out, visit_state_out, relation_out, relation_state_out,
 ):
     f32 = jnp.float32
-    s = lax.axis_index("span")
     home_out[...], home_state_out[...] = adagrad(home_ref[...], home_state_ref[...], home_grad_ref[...], 0)
     visit_out[...], visit_state_out[...] = adagrad(
         visit_ref[...], visit_state_ref[...], visit_grad_ref[...].astype(f32), 0
     )
-    res, ims = [], []
-    for c in range(4):
-        part = quarter_ref[c]
-        own = jnp.zeros((QROWS, 32), f32)
-        for k in range(4):
-            own = jnp.where(s == k, part[:, 32 * k : 32 * (k + 1)], own)
-        res.append(own[:QPART])
-        ims.append(own[QIM : QIM + QPART])
-    grad = jnp.concatenate(res + ims, axis=0)
-    state = relation_state_ref[...] + jnp.sum(grad * grad, axis=0, keepdims=True)[:, :OWN_RELS] * (1.0 / grad.shape[0])
-    step = grad[:, :OWN_RELS] / (jnp.sqrt(state) + ADAGRAD_EPS)
-    step = jnp.concatenate([step, jnp.zeros((grad.shape[0], 32 - OWN_RELS), f32)], axis=1).T[:OWN_RELS]
-    relation_out[...] = relation_ref[...] - LEARN_RATE * step
-    relation_state_out[...] = state
+    grad = jnp.concatenate(
+        [quarter_ref[c][:, first : first + QPART] for first in (0, QIM) for c in range(4)], axis=1
+    )[:OWN_RELS]
+    diagonal = lax.broadcasted_iota(jnp.int32, (OWN_RELS, OWN_RELS), 0) == lax.broadcasted_iota(
+        jnp.int32, (OWN_RELS, OWN_RELS), 1
+    )
+    state = jnp.sum(jnp.where(diagonal, relation_state_ref[...], 0.0), axis=1, keepdims=True)
+    relation_out[...], state = adagrad(relation_ref[...], state, grad, 1)
+    relation_state_out[...] = jnp.sum(jnp.where(diagonal, state, 0.0), axis=0, keepdims=True)
 
 
 def update(*arrays):

time: 101 us -> 94.2 us (0.933); the launches traced: 99.3 us -> 93.6 us
  Pallas kernels: 98 us -> 92.3 us
    pallas_call x1, Pallas kernels: 95 us -> 89.7 us  [bucket_round(): pl.pallas_call(round_kernel, out_shape=(jax.ShapeDtypeStruct(home.shape,...]
where the time goes in v4:
time: 94.2 us; the launch traced here: 93.6 us
  Pallas kernels  92.3 us (98%)
  between operations  1.29 us (1%)
    pallas_call x1, Pallas kernels, bucket_round(): pl.pallas_call(round_kernel, out_shape=(jax.ShapeDtypeStruct(home.shape,...  89.7 us
    pallas_call x1, Pallas kernels, update(): pl.pallas_call(update_kernel, out_shape=tuple((shape(arrays[i]) for i in...  2.54 us

profile of v4, /device:TPU:1, one launch (start us, length us, event | category | flops | bytes accessed | tf_op | source)
XLA Modules:
  0.0 93.6 jit_solution(15518406920191421693)
XLA Ops:
  1.3 89.7 %bucket_round.1 = (f32[400,256]{1,0:T(8,128)}, f32[400,256]{1,0:T(8,128)}, f32[1,256]{1,0:T(1,128)}, bf16[400,256]{1,0:T(8,128)(2,1)}, f32[4,32,128]{2,1,0:T(8,128)}) custom-call(s32[1,1024]{1,0:T(1,128)} %bitcast.13, s32[1,1024]{1,0:T(1,128)} %bitcast.14, s32[1,1024]{1,0:T(1,128)} %bitcast.15, s32[1,1]{1,0:T(1,128)S(6)} %copy.17.count_ref, ...), custom_call_target="tpu_custom_call" | custom-call | tf_op jit(solution)/shard_map/bucket_round/pallas_call | solution.py:505
  91.0 2.5 %update.1 = (f32[400,256]{1,0:T(8,128)}, f32[1,256]{1,0:T(1,128)}, f32[400,256]{1,0:T(8,128)}, f32[1,256]{1,0:T(1,128)}, f32[29,400]{1,0:T(8,128)}, /*index=5*/f32[1,29]{1,0:T(1,128)}) custom-call(f32[400,256]{1,0:T(8,128)} %get-tuple-element.17.home_grad_ref, f32[400,256]{1,0:T(8,128)} %home_ref.3, f32[1,256]{1,0:T(1,128)} %bitcast.17, ...), custom_call_target="tpu_custom_call" | custom-call | tf_op jit(solution)/shard_map/update/pallas_call | solution.py:573

commit v5 on v4

--- a/solution.py
+++ b/solution.py
@@ -79,10 +79,10 @@
 
 def round_kernel(
     src_ref, rel_ref, dst_ref, count_ref, neg_ref, home_ref, visit_ref, visit_state_ref, relation_ref,
-    home_grad_ref, visit_out, visit_state_out, visit_grad_ref, quarter_ref,
+    home_grad_ref, visit_out, visit_state_out, quarter_ref,
     low, low_all, piece, got_piece, index, table, low_hot, hot, total, mine, picked,
     hot_neg, negatives, rel_grad, rel_got, both, grads,
-    r_buf, r_got, l_buf, l_got, row_sum, x_got, x_sum, y_got, q_buf, m_got, o_buf, o_got, visit_sum,
+    r_buf, r_got, l_buf, l_got, row_sum, x_got, x_sum, y_got, q_buf, m_got, o_buf, o_got, moved, moved_state,
     negatives_t, kept, cast, x_in, one_buf, one_got,
     i_send, i_recv, p_send, p_recv, h_send, h_recv, y_send, y_recv, x_send, x_recv,
     r_send, r_recv, l_send, l_recv, k_send, k_recv, v_send, v_recv, a_send, a_recv,
@@ -118,6 +118,21 @@
         pad = jnp.zeros((32, QIM - QPART), f32)
         rest = jnp.zeros((32, 128 - QIM - QPART), f32)
         piece[c] = jnp.concatenate([re, pad, im, rest], axis=1).astype(bf16)
+    greeted(peers)
+    started = []
+
+    def go(copy):
+        copy.start()
+        started.append(copy)
+        return copy
+
+    def to_span(src_of, dst, send, recv):
+        return [
+            go(remote(src_of(lax.rem(s + d, 4)), dst, send.at[d - 1], recv.at[d - 1], span_peers[d - 1]))
+            for d in (1, 2, 3)
+        ]
+
+    pieces = to_span(lambda peer: piece.at[peer], got_piece.at[s], p_send, p_recv)
     rel = rel_ref[...]
     owner = jnp.right_shift(rel * 4520, 17)
     index[s] = jnp.concatenate(
@@ -130,24 +145,6 @@
         ],
         axis=0,
     )
-    low[0] = home_ref[...].astype(bf16)
-    low[1] = visit_ref[...].astype(bf16)
-    low_all[s] = low[...]
-    greeted(peers)
-    started = []
-
-    def go(copy):
-        copy.start()
-        started.append(copy)
-        return copy
-
-    def to_span(src_of, dst, send, recv):
-        return [
-            go(remote(src_of(lax.rem(s + d, 4)), dst, send.at[d - 1], recv.at[d - 1], span_peers[d - 1]))
-            for d in (1, 2, 3)
-        ]
-
-    pieces = to_span(lambda peer: piece.at[peer], got_piece.at[s], p_send, p_recv)
     lists = to_span(lambda peer: index.at[s], index.at[s], i_send, i_recv)
     got_piece[s] = piece[s]
     for copy in pieces:
@@ -161,6 +158,9 @@
     x_copies = [
         go(remote(own, own, x_send.at[d - 1], x_recv.at[d - 1], x_peers[d - 1])) for d in (1, 2, 3)
     ]
+    low[0] = home_ref[...].astype(bf16)
+    low[1] = visit_ref[...].astype(bf16)
+    low_all[s] = low[...]
     lows = [[], []]
     for k in (0, 1):
         for number, peer in enumerate((across, mate)):
@@ -270,10 +270,6 @@
         mine[c] = total[:, c * SHARE : (c + 1) * SHARE].astype(bf16)
     picks = to_span(lambda peer: mine.at[peer], picked.at[s], k_send, k_recv)
     picked[s] = mine[s]
-    moves = [
-        go(remote(visit_ref, visit_out, v_send.at[0], v_recv.at[0], after)),
-        go(remote(visit_state_ref, visit_state_out, v_send.at[1], v_recv.at[1], after)),
-    ]
 
     for copy in lows[0][1:]:
         copy.wait_recv()
@@ -326,6 +322,15 @@
     visit_grad = lax.dot_general(dest_high, hot_dest, NT, preferred_element_type=f32) + lax.dot_general(
         dest_low, hot_dest, NT, preferred_element_type=f32
     )
+    m_copies = {}
+
+    def to_mate(k):
+        for i, row in ((1, across_mate), (0, mate_span)):
+            m_copies[(i, k)] = go(remote(grads.at[row, k], m_got.at[i, k], m_send.at[i, k], m_recv.at[i, k], mate))
+
+    for c in range(4):
+        grads[c, 1] = visit_grad[:, c * 256 : (c + 1) * 256]
+    to_mate(1)
     share = jnp.dot(hot_neg[...], weight, preferred_element_type=f32) + pos_weight * hot_source.astype(f32)
     share_high, share_low = halves(share)
     home_grad = lax.dot_general(trans, share_high, NT, preferred_element_type=f32) + lax.dot_general(
@@ -333,7 +338,7 @@
     )
     for c in range(4):
         grads[c, 0] = home_grad[:, c * 256 : (c + 1) * 256]
-        grads[c, 1] = visit_grad[:, c * 256 : (c + 1) * 256]
+    to_mate(0)
 
     def take(i):
         for copy in swaps[i]:
@@ -360,7 +365,7 @@
                 (r_buf, r_got, rr_send, rr_recv) if way == "r" else (l_buf, l_got, ll_send, ll_recv)
             )
             if dist < 4 or value is None:
-                value = scatter(0, zz, dist < 4)
+                value = scatter(0, zz, dist < 3)
             for part in (0, 1):
                 if dist > FAR[(way, part)]:
                     continue
@@ -417,12 +422,7 @@
                 )
             )
 
-    m_copies = {}
     o_copies = {}
-
-    def to_mate(k):
-        for i, row in ((1, across_mate), (0, mate_span)):
-            m_copies[(i, k)] = go(remote(grads.at[row, k], m_got.at[i, k], m_send.at[i, k], m_recv.at[i, k], mate))
 
     def cross(k):
         m_copies[(1, k)].wait_recv()
@@ -437,25 +437,22 @@
     take(0)
     sow(4, z + 4, False)
     ring(4)
-    to_mate(1)
-    take(1)
-    sow(3, z + 3)
-    sow(7, z - 3)
+    cross(1)
+    sow(3, z + 3, False)
+    sow(7, z - 3, False)
     ring(3)
     ring_row(4)
-    to_mate(0)
+    take(1)
+    cross(0)
     sow(2, z + 2)
     sow(6, z - 2)
     ring(2)
     ring_row(3)
-    cross(1)
     sow(1, z + 1)
     sow(5, z - 1)
     ring(1)
     ring_row(2)
-    cross(0)
-    visit_sum[...] = summed(1).astype(bf16)
-    moves.append(go(remote(visit_sum, visit_grad_ref, v_send.at[2], v_recv.at[2], after)))
+    moved[...], moved_state[...] = adagrad(visit_ref[...], visit_state_ref[...], summed(1), 0)
     sow(0, z)
     ring_row(1)
     near = scatter(0, z)
@@ -475,6 +472,10 @@
         )
         for d in (1, 2, 3)
     ]
+    moves = [
+        go(remote(moved, visit_out, v_send.at[0], v_recv.at[0], after)),
+        go(remote(moved_state, visit_state_out, v_send.at[1], v_recv.at[1], after)),
+    ]
     for way in ("r", "l"):
         back[("other", way, 1)].wait_recv()
     x_sum[...] = reap(0) + one_got[0, 0] + one_got[1, 0]
@@ -508,11 +509,10 @@
             jax.ShapeDtypeStruct(home.shape, f32),
             jax.ShapeDtypeStruct(visit.shape, f32),
             jax.ShapeDtypeStruct(visit_state.shape, f32),
-            jax.ShapeDtypeStruct(visit.shape, bf16),
             jax.ShapeDtypeStruct((4, 32, 128), f32),
         ),
         in_specs=[VMEM] * 9,
-        out_specs=(VMEM,) * 5,
+        out_specs=(VMEM,) * 4,
         scratch_shapes=[
             pltpu.VMEM(pair, bf16), pltpu.VMEM((4,) + pair, bf16),
             pltpu.VMEM((4, 32, 128), bf16), pltpu.VMEM((4, 32, 128), bf16),
@@ -526,7 +526,7 @@
             pltpu.VMEM((4, QROWS, 128), f32), pltpu.VMEM((3, QROWS, 128), f32),
             pltpu.VMEM((QROWS, 128), f32), pltpu.VMEM((QROWS, 128), f32), pltpu.VMEM((4, 32, 128), f32),
             pltpu.VMEM((2,) + pair, f32), pltpu.VMEM(pair, bf16), pltpu.VMEM(pair, bf16),
-            pltpu.VMEM(visit.shape, bf16),
+            pltpu.VMEM(visit.shape, f32), pltpu.VMEM(visit_state.shape, f32),
             pltpu.VMEM((1024, rows), bf16), pltpu.VMEM((8, 4, QROWS, 128), f32), pltpu.VMEM((8, 4, QROWS, 128), bf16),
             pltpu.VMEM((8, 3, QROWS, 128), bf16), lone, lone,
             dma((3,)), dma((3,)), dma((3,)), dma((3,)), dma((2, 3)), dma((2, 3)), dma, dma,
@@ -548,15 +548,14 @@
 
 
 def update_kernel(
-    home_grad_ref, home_ref, home_state_ref, visit_grad_ref, visit_ref, visit_state_ref,
+    home_grad_ref, home_ref, home_state_ref, visit_ref, visit_state_ref,
     quarter_ref, relation_ref, relation_state_ref,
     home_out, home_state_out, visit_out, visit_state_out, relation_out, relation_state_out,
 ):
     f32 = jnp.float32
     home_out[...], home_state_out[...] = adagrad(home_ref[...], home_state_ref[...], home_grad_ref[...], 0)
-    visit_out[...], visit_state_out[...] = adagrad(
-        visit_ref[...], visit_state_ref[...], visit_grad_ref[...].astype(f32), 0
-    )
+    visit_out[...] = visit_ref[...]
+    visit_state_out[...] = visit_state_ref[...]
     grad = jnp.concatenate(
         [quarter_ref[c][:, first : first + QPART] for first in (0, QIM) for c in range(4)], axis=1
     )[:OWN_RELS]
@@ -572,8 +571,8 @@
     shape = lambda a: jax.ShapeDtypeStruct(a.shape, jnp.float32)
     return pl.pallas_call(
         update_kernel,
-        out_shape=tuple(shape(arrays[i]) for i in (1, 2, 4, 5, 7, 8)),
-        in_specs=[VMEM] * 9,
+        out_shape=tuple(shape(arrays[i]) for i in (1, 2, 3, 4, 6, 7)),
+        in_specs=[VMEM] * 8,
         out_specs=(VMEM,) * 6,
         compiler_params=params(),
         name="update",
@@ -584,12 +583,12 @@
     home_table, home_state, visit_table, visit_state, relation_table, relation_state,
     edge_src, edge_rel, edge_dst, edge_count, neg_rows,
 ):
-    home_grad, moved, moved_state, moved_grad, quarters = bucket_round(
+    home_grad, moved, moved_state, quarters = bucket_round(
         edge_src[0], edge_rel[0], edge_dst[0], edge_count, neg_rows,
         home_table, visit_table, visit_state[None], relation_table.T,
     )
     new_home, new_home_state, new_visit, new_visit_state, new_relation, new_relation_state = update(
-        home_grad, home_table, home_state[None], moved_grad, moved, moved_state,
+        home_grad, home_table, home_state[None], moved, moved_state,
         quarters, relation_table.T, relation_state[None],
     )
     return (new_home, new_home_state[0], new_visit, new_visit_state[0], new_relation.T, new_relation_state[0])

time: 94.2 us -> 89.8 us (0.953)
  Pallas kernels: 92.3 us -> 88.4 us
    pallas_call x1, Pallas kernels: 89.7 us -> 86 us  [bucket_round(): pl.pallas_call(round_kernel, out_shape=(jax.ShapeDtypeStruct(home.shape,...]
where the time goes in v5:
time: 89.8 us; the launch traced here: 89.7 us
  Pallas kernels  88.4 us (98%)
  between operations  1.29 us (1%)
    pallas_call x1, Pallas kernels, bucket_round(): pl.pallas_call(round_kernel, out_shape=(jax.ShapeDtypeStruct(home.shape,...  86 us
    pallas_call x1, Pallas kernels, update(): pl.pallas_call(update_kernel, out_shape=tuple((shape(arrays[i]) for i in...  2.37 us

profile of v5, /device:TPU:1, one launch (start us, length us, event | category | flops | bytes accessed | tf_op | source)
XLA Modules:
  0.0 89.7 jit_solution(15896329693911051169)
XLA Ops:
  1.3 86.0 %bucket_round.1 = (f32[400,256]{1,0:T(8,128)}, f32[400,256]{1,0:T(8,128)}, f32[1,256]{1,0:T(1,128)}, f32[4,32,128]{2,1,0:T(8,128)}) custom-call(s32[1,1024]{1,0:T(1,128)} %bitcast.13, s32[1,1024]{1,0:T(1,128)} %bitcast.14, s32[1,1024]{1,0:T(1,128)} %bitcast.15, s32[1,1]{1,0:T(1,128)S(6)} %copy.17.count_ref, s32[1,1024]{1,0:T(1,128)} %neg_ref.1, ...), custom_call_target="tpu_custom_call" | custom-call | tf_op jit(solution)/shard_map/bucket_round/pallas_call | solution.py:506
  87.3 2.4 %update.1 = (f32[400,256]{1,0:T(8,128)}, f32[1,256]{1,0:T(1,128)}, f32[400,256]{1,0:T(8,128)}, f32[1,256]{1,0:T(1,128)}, f32[29,400]{1,0:T(8,128)}, /*index=5*/f32[1,29]{1,0:T(1,128)}) custom-call(f32[400,256]{1,0:T(8,128)} %get-tuple-element.16.home_grad_ref, f32[400,256]{1,0:T(8,128)} %home_ref.3, f32[1,256]{1,0:T(1,128)} %bitcast.16, ...), custom_call_target="tpu_custom_call" | custom-call | tf_op jit(solution)/shard_map/update/pallas_call | solution.py:572

commit v6 on v5

--- a/solution.py
+++ b/solution.py
@@ -209,7 +209,7 @@
         total[...] += jnp.dot(block, hot[...], preferred_element_type=f32)
 
     flying = {}
-    turns = {"r": 4, "l": 3}
+    turns = {"r": 3, "l": 4}
     rows = {}
 
     def pass_on(way, step, key, send, recv, ref):
@@ -239,7 +239,7 @@
                 send, recv = (b_send, b_recv) if way == "r" else (c_send, c_recv)
                 pass_on(way, step, "other", send.at[step], recv.at[step], ref)
             if 1 <= step <= turns[way]:
-                along_x(step if way == "r" else 4 + step, ref)
+                along_x(step if way == "r" else 3 + step, ref)
         if step == 0:
             for copy in x_copies:
                 copy.wait_recv()
@@ -262,10 +262,10 @@
                 gather_row(0, z)
             else:
                 gather_row(step - 1, z - step + 1)
-                gather_row(step + 3, z + step - 1)
+                gather_row(step + 2, z + step - 1)
         if step in (1, 2):
             relay(step - 1)
-    gather_row(4, z - 4)
+    gather_row(7, z + 4)
     for c in range(4):
         mine[c] = total[:, c * SHARE : (c + 1) * SHARE].astype(bf16)
     picks = to_span(lambda peer: mine.at[peer], picked.at[s], k_send, k_recv)
@@ -410,7 +410,7 @@
         for i, way in enumerate(("r", "l")):
             if dist > turns[way]:
                 continue
-            value = reap(dist if way == "r" else 4 + dist)
+            value = reap(dist if way == "r" else 3 + dist)
             if dist < turns[way]:
                 back[("other", way, dist + 1)].wait_recv()
                 value = value + one_got[i, dist]
@@ -435,21 +435,21 @@
         return grads[s, k] + m_got[0, k] + o_got[k].astype(f32)
 
     take(0)
-    sow(4, z + 4, False)
     ring(4)
+    sow(7, z - 4, False)
     cross(1)
     sow(3, z + 3, False)
-    sow(7, z - 3, False)
+    sow(6, z - 3, False)
     ring(3)
     ring_row(4)
     take(1)
     cross(0)
     sow(2, z + 2)
-    sow(6, z - 2)
+    sow(5, z - 2)
     ring(2)
     ring_row(3)
     sow(1, z + 1)
-    sow(5, z - 1)
+    sow(4, z - 1)
     ring(1)
     ring_row(2)
     moved[...], moved_state[...] = adagrad(visit_ref[...], visit_state_ref[...], summed(1), 0)

time: 89.8 us -> 91.1 us (1.014)
  Pallas kernels: 88.4 us -> 89.7 us
    pallas_call x1, Pallas kernels: 86 us -> 87.3 us  [bucket_round(): pl.pallas_call(round_kernel, out_shape=(jax.ShapeDtypeStruct(home.shape,...]
where the time goes in v6:
time: 91.1 us; the launch traced here: 91 us
  Pallas kernels  89.7 us (98%)
  between operations  1.29 us (1%)
    pallas_call x1, Pallas kernels, bucket_round(): pl.pallas_call(round_kernel, out_shape=(jax.ShapeDtypeStruct(home.shape,...  87.3 us
    pallas_call x1, Pallas kernels, update(): pl.pallas_call(update_kernel, out_shape=tuple((shape(arrays[i]) for i in...  2.37 us

profile of v6, /device:TPU:1, one launch (start us, length us, event | category | flops | bytes accessed | tf_op | source)
XLA Modules:
  0.0 91.0 jit_solution(10535269295157545788)
XLA Ops:
  1.3 87.3 %bucket_round.1 = (f32[400,256]{1,0:T(8,128)}, f32[400,256]{1,0:T(8,128)}, f32[1,256]{1,0:T(1,128)}, f32[4,32,128]{2,1,0:T(8,128)}) custom-call(s32[1,1024]{1,0:T(1,128)} %bitcast.13, s32[1,1024]{1,0:T(1,128)} %bitcast.14, s32[1,1024]{1,0:T(1,128)} %bitcast.15, s32[1,1]{1,0:T(1,128)S(6)} %copy.17.count_ref, s32[1,1024]{1,0:T(1,128)} %neg_ref.1, ...), custom_call_target="tpu_custom_call" | custom-call | tf_op jit(solution)/shard_map/bucket_round/pallas_call | solution.py:506
  88.6 2.4 %update.1 = (f32[400,256]{1,0:T(8,128)}, f32[1,256]{1,0:T(1,128)}, f32[400,256]{1,0:T(8,128)}, f32[1,256]{1,0:T(1,128)}, f32[29,400]{1,0:T(8,128)}, /*index=5*/f32[1,29]{1,0:T(1,128)}) custom-call(f32[400,256]{1,0:T(8,128)} %get-tuple-element.16.home_grad_ref, f32[400,256]{1,0:T(8,128)} %home_ref.3, f32[1,256]{1,0:T(1,128)} %bitcast.16, ...), custom_call_target="tpu_custom_call" | custom-call | tf_op jit(solution)/shard_map/update/pallas_call | solution.py:572
